TPU v7x, 512 devices: a whole 4x8x8 slice. The times are simulated.
512 devices in a mesh: dap: 128 (over z_lo, y, x, core), dp: 4 (over z_hi).
Axes of the slice: x: 4, y: 8, z: 8 (z_hi: 4, z_lo: 2; z = z_hi * 2 + z_lo), core: 2. Of those that a mesh axis runs over, the one named last changes fastest.
Arguments:
- pair: bfloat16 [1024, 256, 128], P(('dp', 'dap')), parts along dimension 0, may hold values from -6 to 6
- pair_mask: int32 [1024, 256], P(('dp', 'dap')), parts along dimension 0, may hold values from 0 to 1, as said below
- w_left: bfloat16 [128, 256], replicated, may hold values from -0.5 to 0.5
- w_right: bfloat16 [128, 256], replicated, may hold values from -0.5 to 0.5
- w_tri_gate: bfloat16 [128, 128], replicated, may hold values from -0.5 to 0.5
- w_tri_out: bfloat16 [128, 128], replicated, may hold values from -0.5 to 0.5
- w_attend: bfloat16 [128, 512], replicated, may hold values from -0.5 to 0.5
- w_bias: bfloat16 [128, 4], replicated
- w_att_out: bfloat16 [128, 128], replicated, may hold values from -0.5 to 0.5
Outputs:
- pair_out: float32 [1024, 256, 128], P('dp', 'dap'), parts along dimension 0
There are 4 independent parts, one for each index of `dp`. A program takes and returns all parts, laid end to end along the dimension named above; an argument that names none is the same for every part. Nothing has to cross between parts.
Inputs may be any that keep to these rules, and one draw needn't show every extreme that they name: pair_mask[i, i] = 1 for every residue i.
All inputs are finite; a program needn't handle non-finite values.
Results may differ from a plain program's by a relative error of at most 0.014.
The roundings to bfloat16 on the way count: a program that leaves them out, or rounds other values in their place, can miss the bound.
Values may be sent and summed in bfloat16 or wider, within the bound.
A program may use at most 128 MiB of HBM per device.

v0:
```python
import math

import jax
import jax.numpy as jnp
from jax import lax
from jax.sharding import Mesh
from jax.sharding import PartitionSpec as P

DAP = ("dap_0", "dap_1", "dap_2", "dap_3")
DP_DAP = ("dp", "dap_0", "dap_1", "dap_2", "dap_3")


def from_everyone(value, axis):
    length = lax.axis_size(axis)
    return lax.all_to_all(
        jnp.broadcast_to(value[None], (length, *value.shape)), axis, 0, 0, tiled=True
    )


def joined_along(parts, dim):
    parts = jnp.moveaxis(parts, 0, dim)
    dims = parts.shape
    return parts.reshape(*dims[:dim], dims[dim] * dims[dim + 1], *dims[dim + 2 :])


def whole_of(value, axes, dim):
    far, near = axes
    parts = from_everyone(from_everyone(value, far), near)
    return joined_along(parts.swapaxes(0, 1).reshape(-1, *value.shape), dim)


def in_one_piece(arrays, axis, split_dim, concat_dim, along):
    widths = [math.prod(a.shape[along:]) for a in arrays]
    both = jnp.concatenate(
        [a.reshape(*a.shape[:along], w) for a, w in zip(arrays, widths)], axis=along
    )
    result = lax.all_to_all(both, axis, split_axis=split_dim, concat_axis=concat_dim, tiled=True)
    parts = jnp.split(result, [sum(widths[:k]) for k in range(1, len(widths))], axis=along)
    return tuple(
        (b.reshape(*result.shape[:along], *a.shape[along:]) for a, b in zip(arrays, parts))
    )


def layer_norm(x):
    x = x.astype(jnp.float32)
    mean = jnp.mean(x, axis=-1, keepdims=True)
    var = jnp.mean((x - mean) * (x - mean), axis=-1, keepdims=True)
    return (x - mean) / jnp.sqrt(var + 1e-05)


def matmul(x, w):
    flat = x.reshape(-1, x.shape[-1])
    return jnp.dot(flat, w, preferred_element_type=jnp.float32).reshape(
        x.shape[:-1] + (w.shape[1],)
    )


def edges(zn, weight, maskf, hidden):
    both = matmul(zn, weight)
    return (jax.nn.sigmoid(both[..., :hidden]) * both[..., hidden:] * maskf[..., None]).astype(
        jnp.bfloat16
    )


def triangle_update(pair_part, zn_part, tri, w_tri_gate, w_tri_out):
    tn = layer_norm(tri).astype(jnp.bfloat16)
    update = jax.nn.sigmoid(matmul(zn_part, w_tri_gate)) * matmul(tn, w_tri_out)
    return pair_part.astype(jnp.float32) + update


def attention(pair1, mask_cols, w_attend, w_bias, w_att_out):
    inner = w_att_out.shape[0]
    heads = w_bias.shape[1]
    head_dim = inner // heads
    total, local = (pair1.shape[0], pair1.shape[1])
    yn = layer_norm(pair1).astype(jnp.bfloat16)
    proj = matmul(yn, w_attend)
    query = proj[..., :inner].astype(jnp.bfloat16).reshape(total, local, heads, head_dim)
    keys = proj[..., inner : 2 * inner].astype(jnp.bfloat16).reshape(total, local, heads, head_dim)
    values = (
        proj[..., 2 * inner : 3 * inner].astype(jnp.bfloat16).reshape(total, local, heads, head_dim)
    )
    gate = jax.nn.sigmoid(proj[..., 3 * inner :])
    bias_part = jnp.einsum("kic,ch->hki", yn, w_bias, preferred_element_type=jnp.float32).astype(
        jnp.bfloat16
    )
    bias = whole_of(bias_part, (("dap_0", "dap_1", "dap_2"), "dap_3"), 2)
    scores = jnp.einsum(
        "irhd,krhd->rhki", query, keys, preferred_element_type=jnp.float32
    ) / jnp.sqrt(jnp.float32(head_dim))
    scores = scores + bias.astype(jnp.float32)[None]
    live = jnp.transpose(mask_cols.astype(jnp.float32))[:, None, :, None]
    scores = jnp.where(live > 0.5, scores, jnp.float32(-1000000000.0))
    weights = jax.nn.softmax(scores, axis=2).astype(jnp.bfloat16)
    summed = jnp.einsum(
        "rhki,krhd->irhd", weights, values, preferred_element_type=jnp.float32
    ).reshape(total, local, inner)
    att = (gate * summed).astype(jnp.bfloat16)
    return pair1 + matmul(att, w_att_out)


def shards(pair, pair_mask, w_left, w_right, w_tri_gate, w_tri_out, w_attend, w_bias, w_att_out):
    hidden = w_tri_out.shape[0]
    maskf = pair_mask.astype(jnp.float32)
    zn = layer_norm(pair).astype(jnp.bfloat16)
    left_edge = edges(zn, w_left, maskf, hidden)
    right_edge = edges(zn, w_right, maskf, hidden)
    pair_cols, mask_cols = in_one_piece((pair, pair_mask.astype(jnp.bfloat16)), DAP, 1, 0, 2)
    tri = jnp.einsum(
        "ikc,jkc->ijc",
        lax.all_gather(left_edge, DAP, axis=0, tiled=True),
        right_edge,
        preferred_element_type=jnp.float32,
    )
    zn_cols = layer_norm(pair_cols).astype(jnp.bfloat16)
    pair1 = triangle_update(pair_cols, zn_cols, tri, w_tri_gate, w_tri_out)
    return attention(pair1, mask_cols, w_attend, w_bias, w_att_out)


def solution(mesh):
    torus = Mesh(
        mesh.devices.reshape(2, 8, 4, 2, mesh.shape["dp"]),
        ("dap_0", "dap_1", "dap_2", "dap_3", "dp"),
    )
    placed = (P(DP_DAP, None, None), P(DP_DAP, None), P(), P(), P(), P(), P(), P(), P())
    return jax.shard_map(
        shards, mesh=torus, in_specs=placed, out_specs=P("dp", DAP, None), check_vma=False
    )
```

profile of v0, /device:TPU:1, one launch (start us, length us, event | category | flops | bytes accessed | tf_op | source)
XLA Modules:
  0.0 323.6 jit_solution(5676171652191276352)
XLA Ops:
  6.5 1.1 convert_reduce_fusion.1
  7.6 1.2 fusion.18
  8.8 1.2 fusion.39
  10.0 1.2 fusion.41
  11.3 0.8 fusion.21
  12.5 1.0 pad_maximum_fusion
  13.5 14.2 %all-to-all-start = ((bf16[2,256,129]{2,0,1:T(2,128)(2,1)}), bf16[2,256,129]{2,0,1:T(2,128)(2,1)S(1)}, u32[]{:S(2)}, u32[]{:S(2)}) async-start(bf16[2,256,129]{2,0,1:T(2,128)(2,1)} %pad_maximum_fusion), calls=%async_computation | async-start | bytes 524288 | tf_op jit(solution)/shard_map/all_to_all | solution.py:37
  27.9 15.0 %all-to-all-done = bf16[2,256,129]{2,0,1:T(2,128)(2,1)S(1)} async-done(((bf16[2,256,129]{2,0,1:T(2,128)(2,1)}), bf16[2,256,129]{2,0,1:T(2,128)(2,1)S(1)}, u32[]{:S(2)}, u32[]{:S(2)}) %all-to-all-start) | async-done | bytes 132128 | tf_op jit(solution)/shard_map/all_to_all | solution.py:37
  43.6 0.3 fusion.5
  43.9 207.1 %all-gather.2.cloned.1.call-done = bf16[256,256,128]{2,1,0:T(8,128)(2,1)} async-done(((bf16[2,256,128]{2,1,0:T(8,128)(2,1)}), bf16[256,256,128]{2,1,0:T(8,128)(2,1)}) %all-gather.2.cloned.1.call-update) | async-done | bytes 16777232 | tf_op jit(solution)/shard_map/all_gather | solution.py:111
  251.0 22.1 %copy.147 = bf16[256,256,128]{1,0,2:T(8,128)(2,1)} copy(bf16[256,256,128]{2,1,0:T(8,128)(2,1)} %all-gather.2.cloned.1.call-done) | data formatting | bytes 33554432 | tf_op jit(solution)/shard_map/all_gather | solution.py:111
  273.1 10.2 %fusion.58 = (f32[256,2]{0,1:T(2,128)S(1)}, f32[256,2,128]{0,1,2:T(2,128)S(1)}) fusion(bf16[2,256,128]{1,0,2:T(2,128)(2,1)S(1)} %copy.146, bf16[256,256,128]{1,0,2:T(8,128)(2,1)} %copy.147), kind=kOutput, calls=%fused_computation.85 | convolution fusion | flops 33619456 | bytes 17172480 | tf_op jit(solution)/shard_map/ikc,jkc->ijc/dot_general | solution.py:109
  283.7 0.2 fusion.59
  284.2 0.8 broadcast_in_dim.13
  285.0 9.0 %all-to-all-start.1 = ((bf16[64,4,256,2]{2,1,3,0:T(4,128)(2,1)}), bf16[64,4,256,2]{2,1,3,0:T(4,128)(2,1)S(1)}, u32[]{:S(2)}, u32[]{:S(2)}) async-start(bf16[64,4,256,2]{2,1,3,0:T(4,128)(2,1)} %broadcast_in_dim.13), calls=%async_computation.1 | async-start | bytes 524288 | tf_op jit(solution)/shard_map/all_to_all | solution.py:15
  294.0 0.3 fusion.60
  295.0 9.8 %all-to-all-done.1 = bf16[64,4,256,2]{2,1,3,0:T(4,128)(2,1)S(1)} async-done(((bf16[64,4,256,2]{2,1,3,0:T(4,128)(2,1)}), bf16[64,4,256,2]{2,1,3,0:T(4,128)(2,1)S(1)}, u32[]{:S(2)}, u32[]{:S(2)}) %all-to-all-start.1) | async-done | bytes 262176 | tf_op jit(solution)/shard_map/all_to_all | solution.py:15
  304.9 7.3 %all_to_all.28 = bf16[2,64,4,256,2]{3,2,4,1,0:T(4,128)(2,1)S(1)} all-to-all(bf16[2,64,4,256,2]{3,2,4,1,0:T(4,128)(2,1)S(1)} %broadcast_in_dim.14), channel_id=1, replica_groups=mesh['dap_0'=2,'dap_1'=8,'dap_2'=4,'dap_3'=2,'dp'=4] {'dap_3'}, dimensions={0} | all-to-all | bytes 1048576 | tf_op jit(solution)/shard_map/all_to_all | solution.py:15
  312.4 0.6 copy.157
  312.9 0.3 copy.158
  313.2 0.4 copy.159
  313.6 0.9 fusion.61
  314.5 1.1 fusion.11
  316.0 0.8 copy.162
  (51 shorter events, 3.0 us)
Async XLA Ops:
  6.5 287.5 %copy-start = (bf16[128,512]{1,0:T(8,128)(2,1)S(1)}, bf16[128,512]{1,0:T(8,128)(2,1)}, u32[]{:S(2)}) copy-start(bf16[128,512]{1,0:T(8,128)(2,1)} %param.15) | copy-start | bytes 393220
  6.5 5.6 %copy-start.1 = (bf16[2,256,128]{2,1,0:T(8,128)(2,1)S(1)}, bf16[2,256,128]{2,1,0:T(8,128)(2,1)}, u32[]{:S(2)}) copy-start(bf16[2,256,128]{2,1,0:T(8,128)(2,1)} %param.9) | copy-start | bytes 393220
  6.5 4.7 %copy-start.4 = (s32[2,256]{1,0:T(2,128)S(1)}, s32[2,256]{1,0:T(2,128)}, u32[]{:S(2)}) copy-start(s32[2,256]{1,0:T(2,128)} %param.10) | copy-start | bytes 6148
  6.5 244.5 %all-gather.2.cloned.1.call-start = ((), (), s32[]{:S(2)}) async-start(), calls=%async_computation.3 | async-start | bytes 16908288 | tf_op jit(solution)/shard_map/all_gather | solution.py:111
  12.1 31.5 %copy-start.6 = (bf16[128,128]{1,0:T(8,128)(2,1)S(1)}, bf16[128,128]{1,0:T(8,128)(2,1)}, u32[]{:S(2)}) copy-start(bf16[128,128]{1,0:T(8,128)(2,1)} %param.13) | copy-start | bytes 98308
  13.5 29.3 %all-to-all-start = ((bf16[2,256,129]{2,0,1:T(2,128)(2,1)}), bf16[2,256,129]{2,0,1:T(2,128)(2,1)S(1)}, u32[]{:S(2)}, u32[]{:S(2)}) async-start(bf16[2,256,129]{2,0,1:T(2,128)(2,1)} %pad_maximum_fusion), calls=%async_computation | async-start | bytes 524288 | tf_op jit(solution)/shard_map/all_to_all | solution.py:37
  273.1 10.6 %copy-start.2 = (bf16[128,128]{1,0:T(8,128)(2,1)S(1)}, bf16[128,128]{1,0:T(8,128)(2,1)}, u32[]{:S(2)}) copy-start(bf16[128,128]{1,0:T(8,128)(2,1)} %param.14) | copy-start | bytes 98308
  283.3 0.7 copy-start.5
  285.0 19.8 %all-to-all-start.1 = ((bf16[64,4,256,2]{2,1,3,0:T(4,128)(2,1)}), bf16[64,4,256,2]{2,1,3,0:T(4,128)(2,1)S(1)}, u32[]{:S(2)}, u32[]{:S(2)}) async-start(bf16[64,4,256,2]{2,1,3,0:T(4,128)(2,1)} %broadcast_in_dim.13), calls=%async_computation.1 | async-start | bytes 524288 | tf_op jit(solution)/shard_map/all_to_all | solution.py:15
  314.5 1.2 copy-start.3
Sparse Core Ops, SparseCore 0:
  12.3 238.7 all-gather.1
where the time goes:
time: 325 us; the launch traced here: 324 us
  waiting for transfers between devices  232 us (71%)
  local copies, waits for them, and re-layouts  26.8 us (8%)
  starting transfers between devices  23.2 us (7%)
  matrix products  15.9 us (5%)
  between operations  13.7 us (4%)
  blocking collectives  7.31 us (2%)
  other arithmetic  4.84 us (1%)
    all_gather x1, waiting for transfers between devices, shards(): lax.all_gather(left_edge, DAP, axis=0, tiled=True)  207 us
    all_gather x1, local copies, waits for them, and re-layouts, shards(): lax.all_gather(left_edge, DAP, axis=0, tiled=True)  22.1 us
    all_to_all x1, waiting for transfers between devices, in_one_piece(): lax.all_to_all(both, axis, split_axis=split_dim, concat_axis=concat_dim,...  15 us
    all_to_all x1, starting transfers between devices, in_one_piece(): lax.all_to_all(both, axis, split_axis=split_dim, concat_axis=concat_dim,...  14.2 us
    dot_general x1, matrix products, shards(): jnp.einsum('ikc,jkc->ijc', lax.all_gather(left_edge, DAP, axis=0, tiled=T...  10.2 us
    all_to_all x1, waiting for transfers between devices, from_everyone(): lax.all_to_all(jnp.broadcast_to(value[None], (length, *value.shape)), axi...  9.77 us
    all_to_all x1, starting transfers between devices, from_everyone(): lax.all_to_all(jnp.broadcast_to(value[None], (length, *value.shape)), axi...  9.02 us
    all_to_all x1, blocking collectives, from_everyone(): lax.all_to_all(jnp.broadcast_to(value[None], (length, *value.shape)), axi...  7.31 us
  transfers between devices with their start and end apart: 3, of which 3 were waited for; matrix products, arithmetic and copies ran while one was open for 1% of the time, Pallas kernels for 0%

commit v1 on v0

v1 whole, which is shorter than its diff:
```python
import functools

import jax
import jax.numpy as jnp
from jax import lax
from jax.experimental import pallas as pl
from jax.experimental.pallas import tpu as pltpu
from jax.sharding import PartitionSpec as P

MESH = pl.DeviceIdType.MESH
BF16 = jnp.bfloat16
F32 = jnp.float32
NY = 8
NQ = 16
YN = (((0,), (0,)), ((), ()))
NT = (((1,), (1,)), ((), ()))
TT = (((0,), (1,)), ((), ()))


def device_of(q, y):
    return (q // 8) * 64 + y * 8 + q % 8


def mm(a, b, dims=(((1,), (0,)), ((), ()))):
    return lax.dot_general(a, b, dims, preferred_element_type=F32)


def norm(x, axis):
    mean = jnp.mean(x, axis=axis, keepdims=True)
    d = x - mean
    var = jnp.mean(d * d, axis=axis, keepdims=True)
    return d * lax.rsqrt(var + 1e-05)


def grid_of(n, m):
    return (
        lax.broadcasted_iota(jnp.int32, (n, m), 0),
        lax.broadcasted_iota(jnp.int32, (n, m), 1),
    )


def onehot(cond):
    return jnp.where(cond, F32(1), F32(0)).astype(BF16)


def kernel(
    pair_ref, mask_ref, wl_ref, wr_ref, wg_ref, wo_ref, wa_ref, wb_ref, wao_ref, out_ref,
    send_l, send_r, send_m, got_l, got_r, got_p, got_m,
    next_l, next_r, next_p, have_l, have_r, have_p,
    send_t, got_t, next_t, have_t,
    send_b, got_b, next_b, have_b, scores, ssem, rsem,
):
    me = lax.axis_index("dap")
    zl, y, xc = me // 64, (me // 8) % 8, me % 8
    q = zl * 8 + xc

    barrier = pltpu.get_barrier_semaphore()

    def greet_y(s, c):
        pl.semaphore_signal(barrier, inc=1, device_id={"dap": device_of(q, (y + s) % NY)}, device_id_type=MESH)
        return c

    def greet_q(s, c):
        pl.semaphore_signal(barrier, inc=1, device_id={"dap": device_of((q + s) % NQ, y)}, device_id_type=MESH)
        return c

    lax.fori_loop(1, NY, greet_y, 0)
    lax.fori_loop(1, NQ, greet_q, 0)

    def send_y(src, dst, k):
        def step(s, c):
            to = (y + s) % NY
            pltpu.make_async_remote_copy(
                src_ref=src(to), dst_ref=dst.at[y], send_sem=ssem.at[k], recv_sem=rsem.at[k],
                device_id={"dap": device_of(q, to)}, device_id_type=MESH,
            ).start()
            return c

        lax.fori_loop(1, NY, step, 0)

    def send_q(src, dst, k):
        def step(s, c):
            to = (q + s) % NQ
            pltpu.make_async_remote_copy(
                src_ref=src(to), dst_ref=dst(), send_sem=ssem.at[k], recv_sem=rsem.at[k],
                device_id={"dap": device_of(to, y)}, device_id_type=MESH,
            ).start()
            return c

        lax.fori_loop(1, NQ, step, 0)

    def wait_on(ref, sem):
        pltpu.make_async_copy(ref, ref, sem).wait()

    x = pair_ref[...].astype(F32).reshape(512, 128)
    zn = norm(x, 1).astype(BF16)
    maskf = mask_ref[...].astype(F32)
    mask_row = jnp.concatenate([maskf[0:1], maskf[1:2]], axis=1)

    def edge(w_ref):
        both = mm(w_ref[...], zn, TT)
        return (jax.nn.sigmoid(both[:128]) * both[128:] * mask_row).astype(BF16)

    def put_edge(ref, value):
        for ii in range(2):
            ref[:, ii] = value[:, ii * 256 : (ii + 1) * 256].reshape(NY, 16, 256)

    put_edge(send_l, edge(wl_ref))
    pl.semaphore_wait(barrier, NY + NQ - 2)
    send_y(lambda to: send_l.at[to], got_l, 0)
    put_edge(send_r, edge(wr_ref))
    send_y(lambda to: send_r.at[to], got_r, 1)

    lane, col = grid_of(128, 128)
    rows0 = jnp.where(lane % 2 == 0, maskf[0:1, :128], maskf[0:1, 128:])
    rows1 = jnp.where(lane % 2 == 0, maskf[1:2, :128], maskf[1:2, 128:])
    eye = onehot(lane == col)
    spread = jnp.where(lane < 64, rows0, rows1).astype(BF16)
    send_m[...] = mm(eye, spread, NT).astype(BF16).reshape(NY, 16, 128)
    send_y(lambda to: pair_ref.at[:, :, to], got_p, 2)
    send_y(lambda to: send_m.at[to], got_m, 3)
    got_l[y] = send_l[y]
    got_r[y] = send_r[y]
    got_p[y] = pair_ref[:, :, y]
    got_m[y] = send_m[y]

    r, s = grid_of(256, 256)
    turn = onehot((r // 16 == s % 16) & ((r // 8) % 2 == (s // 16) % 2) & (r % 8 == s // 32))
    back = onehot((s // 16 == r % 16) & ((s // 8) % 2 == (r // 16) % 2) & (s % 8 == r // 32))

    wait_on(got_l.at[pl.ds(0, NY - 1)], rsem.at[0])
    next_l[...] = mm(turn, got_l[...].reshape(256, 256)).astype(BF16).reshape(NQ, 16, 256)
    send_q(lambda to: next_l.at[to], lambda: have_l.at[q], 4)
    wait_on(got_r.at[pl.ds(0, NY - 1)], rsem.at[1])
    next_r[...] = mm(turn, got_r[...].reshape(256, 256)).astype(BF16).reshape(NQ, 16, 256)
    send_q(lambda to: next_r.at[to], lambda: have_r.at[q], 5)
    have_l[q] = next_l[q]
    have_r[q] = next_r[q]

    wait_on(got_p.at[pl.ds(0, NY - 1)], rsem.at[2])
    wait_on(got_m.at[pl.ds(0, NY - 1)], rsem.at[3])
    m0 = got_m[...].astype(F32)
    m1 = pltpu.roll(m0.reshape(128, 128), 64, 1).reshape(NY, 16, 128)
    m01 = jnp.stack([m0, m1], axis=1).reshape(256, 128).astype(BF16)
    m01 = mm(turn, m01).astype(BF16).reshape(8, 2, 16, 128)
    for z in range(2):
        part = mm(turn, got_p[:, :, z].reshape(256, 128)).astype(BF16)
        next_p[z * 8 : z * 8 + 8, 0:2] = part.reshape(8, 2, 16, 128)
        next_p[z * 8 : z * 8 + 8, 2:4] = m01
    send_q(lambda to: next_p.at[to], lambda: have_p.at[q], 6)
    have_p[q] = next_p[q]

    wait_on(have_l.at[pl.ds(0, NQ - 1)], rsem.at[4])
    wait_on(have_r.at[pl.ds(0, NQ - 1)], rsem.at[5])
    tri = mm(have_r[...].reshape(256, 256), have_l[...].reshape(256, 256), NT)
    send_t[...] = tri.astype(BF16).reshape(NQ, 16, 256)
    send_q(lambda to: send_t.at[to], lambda: got_t.at[q], 7)
    got_t[q] = send_t[q]

    wait_on(have_p.at[pl.ds(0, NQ - 1)], rsem.at[6])
    pairs, gates, lives = [], [], []
    pick = onehot(lane == zl)
    for jj in range(2):
        p = have_p[:, jj].reshape(256, 128).astype(F32)
        zc = norm(p, 1).astype(BF16)
        pairs.append(p)
        gates.append(jax.nn.sigmoid(mm(zc, wg_ref[...])))
        lives.append(mm(have_p[:, 2 + jj].reshape(256, 128), pick))
    wa = wa_ref[...]
    wk = wa[:, 128:256]
    wq_t, wv_t, wgate_t = wa[:, :128], wa[:, 256:384], wa[:, 384:]

    wait_on(got_t.at[pl.ds(0, NQ - 1)], rsem.at[7])
    next_t[...] = mm(back, got_t[...].reshape(256, 256)).astype(BF16).reshape(NY, 32, 256)
    send_y(lambda to: next_t.at[to], have_t, 8)
    have_t[y] = next_t[y]
    order = onehot(
        (col // 16 == lane % 8)
        & ((col // 8) % 2 == lane // 64)
        & ((col // 4) % 2 == (lane // 8) % 2)
        & (col % 4 == (lane // 16) % 4)
    )
    wait_on(have_t.at[pl.ds(0, NY - 1)], rsem.at[8])

    pair1, yns = [], []
    for jj in range(2):
        t = have_t[:, jj * 16 : (jj + 1) * 16].reshape(128, 256).astype(F32)
        tn = norm(t, 0).astype(BF16)
        p1 = pairs[jj] + gates[jj] * mm(tn, wo_ref[...], YN)
        pair1.append(p1)
        yns.append(norm(p1, 1).astype(BF16))

    parts = [mm(wb_ref[...], yn, TT) for yn in yns]
    both = jnp.concatenate(parts, axis=0)
    send_b[...] = jnp.concatenate([both[:, :128], both[:, 128:]], axis=0).astype(BF16)
    send_y(lambda to: send_b, got_b, 9)
    got_b[y] = send_b[...]

    keys, queries, values, out_gates = [], [], [], []
    for jj in range(2):
        keys.append(mm(yns[jj], wk).astype(BF16))
        queries.append(mm(wq_t, yns[jj], TT).astype(BF16))
        values.append(mm(wv_t, yns[jj], TT).astype(BF16))
        out_gates.append(jax.nn.sigmoid(mm(wgate_t, yns[jj], TT)))

    wait_on(got_b.at[pl.ds(0, NY - 1)], rsem.at[9])
    next_b[...] = mm(order, got_b[...].reshape(128, 128)).astype(BF16).reshape(8, 16, 128)
    send_q(lambda to: next_b, lambda: have_b.at[q], 10)
    have_b[q] = next_b[...]

    head_row = lax.broadcasted_iota(jnp.int32, (128, 256), 0) // 32
    scale = F32(32.0**-0.5)
    for jj in range(2):
        for h in range(4):
            qh = jnp.where(head_row == h, queries[jj].astype(F32), F32(0)).astype(BF16)
            scores[jj, h] = mm(keys[jj], qh) * scale

    wait_on(have_b.at[pl.ds(0, NQ - 1)], rsem.at[10])
    atts = [[], []]
    for h in range(4):
        bias = jnp.concatenate(
            [mm(eye, have_b[:, kh * 4 + h].reshape(256, 128), NT) for kh in range(2)], axis=0
        )
        for jj in range(2):
            live = jnp.concatenate([lives[jj], lives[jj]], axis=1) > 0.5
            sc = jnp.where(live, scores[jj, h] + bias, F32(-1e9))
            e = jnp.exp(sc - jnp.max(sc, axis=0, keepdims=True))
            w = (e / jnp.sum(e, axis=0, keepdims=True)).astype(BF16)
            o = mm(values[jj][h * 32 : (h + 1) * 32], w)
            atts[jj].append(out_gates[jj][h * 32 : (h + 1) * 32] * o)
    for jj in range(2):
        att = jnp.concatenate(atts[jj], axis=0).astype(BF16)
        res = pair1[jj] + mm(att, wao_ref[...], YN)
        for qq in range(NQ):
            for ii in range(2):
                start = (qq // 8) * 256 + (qq % 8) * 4 + ii * 2 + jj
                out_ref[pl.ds(start, 8, stride=32), :] = res[qq * 16 + ii * 8 : qq * 16 + ii * 8 + 8]

    for k, ref in (
        (0, got_l), (1, got_r), (2, got_p), (3, got_m), (8, have_t), (9, got_b),
    ):
        wait_on(ref.at[pl.ds(0, NY - 1)], ssem.at[k])
    for k, ref in ((4, have_l), (5, have_r), (6, have_p), (7, got_t), (10, have_b)):
        wait_on(ref.at[pl.ds(0, NQ - 1)], ssem.at[k])


def shards(pair, pair_mask, *weights):
    vm = pl.BlockSpec(memory_space=pltpu.VMEM)
    out = pl.pallas_call(
        kernel,
        out_shape=jax.ShapeDtypeStruct((512, 128), F32),
        in_specs=[vm] * 9,
        out_specs=vm,
        scratch_shapes=[
            pltpu.VMEM((NY, 2, 16, 256), BF16),
            pltpu.VMEM((NY, 2, 16, 256), BF16),
            pltpu.VMEM((NY, 16, 128), BF16),
            pltpu.VMEM((NY, 2, 16, 256), BF16),
            pltpu.VMEM((NY, 2, 16, 256), BF16),
            pltpu.VMEM((NY, 2, 2, 16, 128), BF16),
            pltpu.VMEM((NY, 16, 128), BF16),
            pltpu.VMEM((NQ, 16, 256), BF16),
            pltpu.VMEM((NQ, 16, 256), BF16),
            pltpu.VMEM((NQ, 4, 16, 128), BF16),
            pltpu.VMEM((NQ, 16, 256), BF16),
            pltpu.VMEM((NQ, 16, 256), BF16),
            pltpu.VMEM((NQ, 4, 16, 128), BF16),
            pltpu.VMEM((NQ, 16, 256), BF16),
            pltpu.VMEM((NQ, 16, 256), BF16),
            pltpu.VMEM((NY, 32, 256), BF16),
            pltpu.VMEM((NY, 32, 256), BF16),
            pltpu.VMEM((16, 128), BF16),
            pltpu.VMEM((NY, 16, 128), BF16),
            pltpu.VMEM((8, 16, 128), BF16),
            pltpu.VMEM((NQ, 8, 16, 128), BF16),
            pltpu.VMEM((2, 4, 256, 256), F32),
            pltpu.SemaphoreType.DMA((11,)),
            pltpu.SemaphoreType.DMA((11,)),
        ],
        compiler_params=pltpu.CompilerParams(
            collective_id=0, has_side_effects=True, vmem_limit_bytes=32 * 1024 * 1024
        ),
    )(pair.reshape(2, 2, 8, 16, 128), pair_mask, *weights)
    return out.reshape(256, 2, 128)


def solution(mesh):
    rows = ("dp", "dap")
    return jax.shard_map(
        shards,
        mesh=mesh,
        in_specs=(P(rows, None, None), P(rows, None), P(), P(), P(), P(), P(), P(), P()),
        out_specs=P("dp", "dap", None),
        check_vma=False,
    )
```

time: 325 us -> 57.6 us (0.18)
  waiting for transfers between devices: 232 us -> 0 us
  Pallas kernels: 0 us -> 50.6 us
  starting transfers between devices: 23.2 us -> 0 us
  local copies, waits for them, and re-layouts: 26.8 us -> 6.52 us
  matrix products: 15.9 us -> 0 us
  between operations: 13.7 us -> 0.03 us
  blocking collectives: 7.31 us -> 0 us
  other arithmetic: 4.84 us -> 0 us
    all_gather x1 -> x0, waiting for transfers between devices: 207 us -> none  [shards(): lax.all_gather(left_edge, DAP, axis=0, tiled=True)]
    pallas_call x0 -> x1, Pallas kernels: none -> 50.6 us  [shards(): pl.pallas_call(kernel, out_shape=jax.ShapeDtypeStruct((512, 128), F32), i...]
    all_to_all x2 -> x0, waiting for transfers between devices: 24.7 us -> none  [the longest x1 15 us: in_one_piece(): lax.all_to_all(both, axis, split_axis=split_dim, concat_axis=concat_dim,...]
    all_to_all x2 -> x0, starting transfers between devices: 23.2 us -> none  [the longest x1 14.2 us: in_one_piece(): lax.all_to_all(both, axis, split_axis=split_dim, concat_axis=concat_dim,...]
    all_gather x1 -> x0, local copies, waits for them, and re-layouts: 22.1 us -> none  [shards(): lax.all_gather(left_edge, DAP, axis=0, tiled=True)]
    dot_general x9 -> x0, matrix products: 15 us -> none  [the longest x1 10.2 us: shards(): jnp.einsum('ikc,jkc->ijc', lax.all_gather(left_edge, DAP, axis=0, tiled=T...]
    all_to_all x1 -> x0, blocking collectives: 7.31 us -> none  [from_everyone(): lax.all_to_all(jnp.broadcast_to(value[None], (length, *value.shape)), axi...]
    unnamed x18, local copies, waits for them, and re-layouts: 0.51 us -> 6.52 us
  transfers between devices with their start and end apart: 3 -> 0, of which waited for: 3 -> 0; matrix products, arithmetic and copies ran while one was open for 1% -> 0% of each run, Pallas kernels for 0% -> 0%
where the time goes in v1:
time: 57.6 us; the launch traced here: 57.2 us
  Pallas kernels  50.6 us (88%)
  local copies, waits for them, and re-layouts  6.52 us (11%)
    pallas_call x1, Pallas kernels, shards(): pl.pallas_call(kernel, out_shape=jax.ShapeDtypeStruct((512, 128), F32), i...  50.6 us
    unnamed x18, local copies, waits for them, and re-layouts  6.52 us

profile of v1, /device:TPU:1, one launch (start us, length us, event | category | flops | bytes accessed | tf_op | source)
XLA Modules:
  0.0 57.2 jit_solution(7672902328443559390)
XLA Ops:
  0.0 0.0 copy-start.4
  0.0 0.0 copy-start.7
  0.0 0.8 %copy.10.wb_ref = bf16[128,4]{1,0:T(8,128)(2,1)S(1)} copy(bf16[128,4]{0,1:T(4,128)(2,1)} %param.16) | data formatting | bytes 2048 | tf_op args[7]
  0.8 0.0 copy-done.4
  0.8 0.0 copy-done.7
  0.8 0.0 copy-start
  0.8 0.9 %copy-done = bf16[2,256,128]{2,1,0:T(8,128)(2,1)S(1)} copy-done((bf16[2,256,128]{2,1,0:T(8,128)(2,1)S(1)}, bf16[2,256,128]{2,1,0:T(8,128)(2,1)}, u32[]{:S(2)}) %copy-start) | copy-done | bytes 131096
  1.7 0.0 copy-start.1
  1.7 0.9 %copy-done.1 = bf16[128,512]{1,0:T(8,128)(2,1)S(1)} copy-done((bf16[128,512]{1,0:T(8,128)(2,1)S(1)}, bf16[128,512]{1,0:T(8,128)(2,1)}, u32[]{:S(2)}) %copy-start.1) | copy-done | bytes 131096
  2.6 0.0 copy-start.2
  2.6 0.8 %copy-done.2 = bf16[128,256]{1,0:T(8,128)(2,1)S(1)} copy-done((bf16[128,256]{1,0:T(8,128)(2,1)S(1)}, bf16[128,256]{1,0:T(8,128)(2,1)}, u32[]{:S(2)}) %copy-start.2) | copy-done | bytes 65560
  3.5 0.0 copy-start.3
  3.5 0.8 %copy-done.3 = bf16[128,256]{1,0:T(8,128)(2,1)S(1)} copy-done((bf16[128,256]{1,0:T(8,128)(2,1)S(1)}, bf16[128,256]{1,0:T(8,128)(2,1)}, u32[]{:S(2)}) %copy-start.3) | copy-done | bytes 65560
  4.3 0.0 copy-start.5
  4.3 0.8 %copy-done.5 = bf16[128,128]{1,0:T(8,128)(2,1)S(1)} copy-done((bf16[128,128]{1,0:T(8,128)(2,1)S(1)}, bf16[128,128]{1,0:T(8,128)(2,1)}, u32[]{:S(2)}) %copy-start.5) | copy-done | bytes 32792
  5.1 0.0 copy-start.6
  5.1 0.8 %copy-done.6 = bf16[128,128]{1,0:T(8,128)(2,1)S(1)} copy-done((bf16[128,128]{1,0:T(8,128)(2,1)S(1)}, bf16[128,128]{1,0:T(8,128)(2,1)}, u32[]{:S(2)}) %copy-start.6) | copy-done | bytes 32792
  5.8 50.6 %shard_map.91 = f32[512,128]{1,0:T(8,128)S(1)} custom-call(bf16[2,2,8,16,128]{4,3,2,1,0:T(8,128)(2,1)S(1)} %bitcast.3, s32[2,256]{1,0:T(2,128)S(1)} %copy-done.7, bf16[128,256]{1,0:T(8,128)(2,1)S(1)} %copy-done.2, bf16[128,256]{1,0:T(8,128)(2,1)S(1)} %copy-done.3, bf16[128,128]{1,0:T(8,128)(2,1)S(1)} %copy-done.4, bf16[128,128]{1,0:T(8,128)(2,1)S(1)} %copy-done.5, ...), custom_call_target="tpu_custom_call" | custom-call | tf_op jit(solution)/shard_map/pallas_call | solution.py:249
  56.4 0.7 %copy.12 = f32[256,2,128]{2,1,0:T(2,128)} copy(f32[256,2,128]{2,1,0:T(2,128)S(1)} %bitcast.2) | data formatting | bytes 524288
Async XLA Ops:
  0.0 0.8 %copy-start.4 = (bf16[128,128]{1,0:T(8,128)(2,1)S(1)}, bf16[128,128]{1,0:T(8,128)(2,1)}, u32[]{:S(2)}) copy-start(bf16[128,128]{1,0:T(8,128)(2,1)} %wg_ref.1) | copy-start | bytes 98308
  0.0 0.8 %copy-start.7 = (s32[2,256]{1,0:T(2,128)S(1)}, s32[2,256]{1,0:T(2,128)}, u32[]{:S(2)}) copy-start(s32[2,256]{1,0:T(2,128)} %mask_ref.1) | copy-start | bytes 6148
  0.8 0.9 %copy-start = (bf16[2,256,128]{2,1,0:T(8,128)(2,1)S(1)}, bf16[2,256,128]{2,1,0:T(8,128)(2,1)}, u32[]{:S(2)}) copy-start(bf16[2,256,128]{2,1,0:T(8,128)(2,1)} %param.9) | copy-start | bytes 393220
  1.7 0.9 %copy-start.1 = (bf16[128,512]{1,0:T(8,128)(2,1)S(1)}, bf16[128,512]{1,0:T(8,128)(2,1)}, u32[]{:S(2)}) copy-start(bf16[128,512]{1,0:T(8,128)(2,1)} %wa_ref.1) | copy-start | bytes 393220
  2.6 0.8 %copy-start.2 = (bf16[128,256]{1,0:T(8,128)(2,1)S(1)}, bf16[128,256]{1,0:T(8,128)(2,1)}, u32[]{:S(2)}) copy-start(bf16[128,256]{1,0:T(8,128)(2,1)} %wl_ref.1) | copy-start | bytes 196612
  3.5 0.8 %copy-start.3 = (bf16[128,256]{1,0:T(8,128)(2,1)S(1)}, bf16[128,256]{1,0:T(8,128)(2,1)}, u32[]{:S(2)}) copy-start(bf16[128,256]{1,0:T(8,128)(2,1)} %wr_ref.1) | copy-start | bytes 196612
  4.3 0.8 %copy-start.5 = (bf16[128,128]{1,0:T(8,128)(2,1)S(1)}, bf16[128,128]{1,0:T(8,128)(2,1)}, u32[]{:S(2)}) copy-start(bf16[128,128]{1,0:T(8,128)(2,1)} %wo_ref.1) | copy-start | bytes 98308
  5.1 0.8 %copy-start.6 = (bf16[128,128]{1,0:T(8,128)(2,1)S(1)}, bf16[128,128]{1,0:T(8,128)(2,1)}, u32[]{:S(2)}) copy-start(bf16[128,128]{1,0:T(8,128)(2,1)} %wao_ref.1) | copy-start | bytes 98308

commit v2 on v1

v2 whole, which is shorter than its diff:
```python
import functools

import jax
import jax.numpy as jnp
from jax import lax
from jax.experimental import pallas as pl
from jax.experimental.pallas import tpu as pltpu
from jax.sharding import PartitionSpec as P

MESH = pl.DeviceIdType.MESH
BF16 = jnp.bfloat16
F32 = jnp.float32
NY = 8
NQ = 16
YN = (((0,), (0,)), ((), ()))
NT = (((1,), (1,)), ((), ()))
TT = (((0,), (1,)), ((), ()))


FAR_Y = (4, 3, 5, 2, 6, 1, 7)
FAR_Q = tuple((dz, dx, dc) for dz, dx in ((1, 2), (1, 1), (1, 3), (0, 2), (0, 1), (0, 3), (1, 0)) for dc in (0, 1)) + ((0, 0, 1),)
FAR_CHIP = tuple(step for step in FAR_Q if step[2] == 0)


def device_of(q, y):
    return (q // 8) * 64 + y * 8 + q % 8


def moved(q, step):
    dz, dx, dc = step
    return ((q // 8 + dz) % 2) * 8 + ((q // 2 + dx) % 4) * 2 + (q + dc) % 2


def mm(a, b, dims=(((1,), (0,)), ((), ()))):
    return lax.dot_general(a, b, dims, preferred_element_type=F32)


def norm(x, axis):
    mean = jnp.mean(x, axis=axis, keepdims=True)
    d = x - mean
    var = jnp.mean(d * d, axis=axis, keepdims=True)
    return d * lax.rsqrt(var + 1e-05)


def grid_of(n, m):
    return (
        lax.broadcasted_iota(jnp.int32, (n, m), 0),
        lax.broadcasted_iota(jnp.int32, (n, m), 1),
    )


def onehot(cond):
    return jnp.where(cond, F32(1), F32(0)).astype(BF16)


def kernel(
    pair_in, mask_in, wl_in, wr_in, wg_in, wo_in, wa_in, wb_in, wao_in, out_ref,
    pair_ref, mask_ref, wl_ref, wr_ref, wg_ref, wo_ref, wa_ref, wb_ref, wao_ref,
    send_l, send_r, send_m, got_l, got_r, got_p, got_m,
    next_l, next_r, next_p, have_l, have_r, have_p,
    send_t, got_t, next_t, have_t,
    send_b, got_b, next_b, have_b, scores, ssem, rsem, lsem,
):
    me = lax.axis_index("dap")
    zl, y, xc = me // 64, (me // 8) % 8, me % 8
    q = zl * 8 + xc

    loads = [
        pltpu.make_async_copy(a, b, lsem.at[k])
        for k, (a, b) in enumerate((
            (pair_in, pair_ref), (wl_in, wl_ref), (mask_in, mask_ref), (wr_in, wr_ref), (wg_in, wg_ref),
            (wo_in, wo_ref), (wa_in, wa_ref), (wb_in, wb_ref), (wao_in, wao_ref),
        ))
    ]
    for load in loads:
        load.start()
    barrier = pltpu.get_barrier_semaphore()

    peers = [device_of(q, (y + s) % NY) for s in FAR_Y] + [device_of(moved(q, step), y) for step in FAR_Q]
    for peer in peers:
        pl.semaphore_signal(barrier, inc=1, device_id={"dap": peer}, device_id_type=MESH)

    sent, due = {}, {}

    def send(src, dst, k, peer):
        pltpu.make_async_remote_copy(
            src_ref=src, dst_ref=dst, send_sem=ssem.at[k], recv_sem=rsem.at[k],
            device_id={"dap": peer}, device_id_type=MESH,
        ).start()

    def send_y(src, dst, k):
        sent[k] = due[k] = dst.at[pl.ds(0, NY - 1)]
        for s in FAR_Y:
            to = (y + s) % NY
            send(src(to), dst.at[y], k, device_of(q, to))

    def send_q(src, dst, k):
        sent[k] = due[k] = dst.at[pl.ds(0, NQ - 1)]
        for step in FAR_Q:
            to = moved(q, step)
            send(src(to), dst.at[q], k, device_of(to, y))

    def wait_on(ref, sem):
        pltpu.make_async_copy(ref, ref, sem).wait()

    def arrive(k):
        wait_on(due.pop(k), rsem.at[k])

    for load in loads[:3]:
        load.wait()
    x = pair_ref[...].astype(F32).reshape(512, 128)
    zn = norm(x, 1).astype(BF16)
    maskf = mask_ref[...].astype(F32)
    mask_row = jnp.concatenate([maskf[0:1], maskf[1:2]], axis=1)

    lane, col = grid_of(128, 128)
    by_q = onehot((lane % 16 == col // 8) & (lane // 16 == col % 8))
    q_by = onehot((col % 16 == lane // 8) & (col // 16 == lane % 8))

    def edge(w):
        both = mm(w, zn, TT)
        return jax.nn.sigmoid(both[:128]) * both[128:] * mask_row

    left = edge(wl_ref[...]).astype(BF16)
    for ii in range(2):
        send_l[:, ii] = left[:, ii * 256 : (ii + 1) * 256].reshape(NY, 16, 256)
    pl.semaphore_wait(barrier, NY + NQ - 2)
    send_y(lambda to: send_l.at[to], got_l, 0)
    for load in loads[3:]:
        load.wait()
    wr = jnp.concatenate([mm(wr_ref[:, :128], by_q), mm(wr_ref[:, 128:], by_q)], axis=1).astype(BF16)
    right = edge(wr)
    right = jnp.stack([right[:, :256].reshape(NQ, 8, 256), right[:, 256:].reshape(NQ, 8, 256)], axis=1)
    send_r[...] = right.reshape(NQ, 16, 256).astype(BF16)
    send_q(lambda to: send_r.at[to], got_r, 1)
    got_l[y] = send_l[y]
    got_r[q] = send_r[q]

    r, s = grid_of(256, 256)
    turn = onehot((r // 16 == s % 16) & ((r // 8) % 2 == (s // 16) % 2) & (r % 8 == s // 32))
    back = onehot((s // 16 == r % 16) & ((s // 8) % 2 == (r // 16) % 2) & (s % 8 == r // 32))

    arrive(1)
    next_r[...] = mm(back, got_r[...].reshape(256, 256)).astype(BF16).reshape(NY, 32, 256)
    send_y(lambda to: next_r.at[to], have_r, 5)
    arrive(0)
    next_l[...] = mm(turn, got_l[...].reshape(256, 256)).astype(BF16).reshape(NQ, 16, 256)
    send_q(lambda to: next_l.at[to], have_l, 4)
    have_l[q] = next_l[q]
    have_r[y] = next_r[y]

    rows0 = jnp.where(lane % 2 == 0, maskf[0:1, :128], maskf[0:1, 128:])
    rows1 = jnp.where(lane % 2 == 0, maskf[1:2, :128], maskf[1:2, 128:])
    eye = onehot(lane == col)
    spread = jnp.where(lane < 64, rows0, rows1).astype(BF16)
    send_m[...] = mm(eye, spread, NT).astype(BF16).reshape(NY, 16, 128)
    send_y(lambda to: pair_in.at[:, :, to], got_p, 2)
    send_y(lambda to: send_m.at[to], got_m, 3)
    got_p[y] = pair_ref[:, :, y]
    got_m[y] = send_m[y]

    arrive(5)
    arrive(4)
    tri = mm(have_r[...].reshape(256, 256), have_l[...].reshape(256, 256), NT)
    send_t[...] = tri.astype(BF16).reshape(NY, 32, 256)
    send_y(lambda to: send_t.at[to], got_t, 7)
    got_t[y] = send_t[y]

    arrive(2)
    arrive(3)
    m0 = got_m[...].astype(F32)
    m1 = pltpu.roll(m0.reshape(128, 128), 64, 1).reshape(NY, 16, 128)
    m01 = jnp.stack([m0, m1], axis=1).reshape(256, 128).astype(BF16)
    m01 = mm(turn, m01).astype(BF16).reshape(8, 2, 16, 128)
    for z in range(2):
        part = mm(turn, got_p[:, :, z].reshape(256, 128)).astype(BF16)
        next_p[z * 8 : z * 8 + 8, 0:2] = part.reshape(8, 2, 16, 128)
        next_p[z * 8 : z * 8 + 8, 2:4] = m01
    send_q(lambda to: next_p.at[to], have_p, 6)
    have_p[q] = next_p[q]

    arrive(6)
    pairs, gates, lives = [], [], []
    pick = onehot(lane == zl)
    for jj in range(2):
        p = have_p[:, jj].reshape(256, 128).astype(F32)
        zc = norm(p, 1).astype(BF16)
        pairs.append(p)
        gates.append(jax.nn.sigmoid(mm(zc, wg_ref[...])))
        lives.append(mm(have_p[:, 2 + jj].reshape(256, 128), pick))
    wa = wa_ref[...]
    wk = wa[:, 128:256]
    wq_t, wv_t, wgate_t = wa[:, :128], wa[:, 256:384], wa[:, 384:]

    arrive(7)
    next_t[...] = mm(turn, got_t[...].reshape(256, 256)).astype(BF16).reshape(NQ, 16, 256)
    send_q(lambda to: next_t.at[to], have_t, 8)
    have_t[q] = next_t[q]
    wo = mm(q_by, wo_ref[...]).astype(BF16)
    order = onehot(
        (col // 16 == lane % 8)
        & ((col // 8) % 2 == lane // 64)
        & ((col // 4) % 2 == (lane // 8) % 2)
        & (col % 4 == (lane // 16) % 4)
    )
    arrive(8)

    pair1, yns = [], []
    tris = have_t[...].astype(F32).reshape(NQ, 2, 8, 256)
    for jj in range(2):
        t = tris[:, jj].reshape(128, 256)
        tn = norm(t, 0).astype(BF16)
        p1 = pairs[jj] + gates[jj] * mm(tn, wo, YN)
        pair1.append(p1)
        yns.append(norm(p1, 1).astype(BF16))

    parts = [mm(wb_ref[...], yn, NT) for yn in yns]
    both = jnp.concatenate(parts, axis=0)
    send_b[...] = jnp.concatenate([both[:, :128], both[:, 128:]], axis=0).astype(BF16)
    send_y(lambda to: send_b, got_b, 9)
    got_b[y] = send_b[...]

    keys, queries, values, out_gates = [], [], [], []
    for jj in range(2):
        keys.append(mm(yns[jj], wk).astype(BF16))
        queries.append(mm(wq_t, yns[jj], TT).astype(BF16))
        values.append(mm(wv_t, yns[jj], TT).astype(BF16))
        out_gates.append(jax.nn.sigmoid(mm(wgate_t, yns[jj], TT)))

    arrive(9)
    next_b[...] = mm(order, got_b[...].reshape(128, 128)).astype(BF16).reshape(8, 16, 128)
    near = moved(q, (0, 0, 1))
    for k, step in enumerate(FAR_CHIP):
        sent[10 + k] = have_b.at[0]
        to = moved(q, step)
        send(next_b, have_b.at[q], 10 + k, device_of(to, y))
    have_b[q] = next_b[...]
    sent[17] = due[17] = have_b.at[pl.ds(0, 8)]
    send(next_b, have_b.at[q], 17, device_of(near, y))

    head_row = lax.broadcasted_iota(jnp.int32, (128, 256), 0) // 32
    scale = F32(32.0**-0.5)
    for jj in range(2):
        for h in range(4):
            qh = jnp.where(head_row == h, queries[jj].astype(F32), F32(0)).astype(BF16)
            scores[jj, h] = mm(keys[jj], qh) * scale

    for k in reversed(range(7)):
        dz, dx, _ = FAR_CHIP[k]
        at = moved(q, (dz, -dx, 0))
        wait_on(have_b.at[0], rsem.at[10 + k])
        send(have_b.at[at], have_b.at[at], 17, device_of(near, y))
    arrive(17)
    atts = [[], []]
    for h in range(4):
        bias = jnp.concatenate(
            [mm(eye, have_b[:, kh * 4 + h].reshape(256, 128), NT) for kh in range(2)], axis=0
        )
        for jj in range(2):
            live = jnp.concatenate([lives[jj], lives[jj]], axis=1) > 0.5
            sc = jnp.where(live, scores[jj, h] + bias, F32(-1e9))
            e = jnp.exp(sc - jnp.max(sc, axis=0, keepdims=True))
            w = (e / jnp.sum(e, axis=0, keepdims=True)).astype(BF16)
            o = mm(values[jj][h * 32 : (h + 1) * 32], w)
            atts[jj].append(out_gates[jj][h * 32 : (h + 1) * 32] * o)
    for jj in range(2):
        att = jnp.concatenate(atts[jj], axis=0).astype(BF16)
        res = pair1[jj] + mm(att, wao_ref[...], YN)
        for qq in range(NQ):
            for ii in range(2):
                start = (qq // 8) * 256 + (qq % 8) * 4 + ii * 2 + jj
                out_ref[pl.ds(start, 8, stride=32), :] = res[qq * 16 + ii * 8 : qq * 16 + ii * 8 + 8]

    for k, ref in sent.items():
        wait_on(ref, ssem.at[k])


def shards(pair, pair_mask, wl, wr, wg, wo, wa, wb, wao):
    vm = pl.BlockSpec(memory_space=pltpu.VMEM)
    hbm = pl.BlockSpec(memory_space=pltpu.HBM)
    out = pl.pallas_call(
        kernel,
        out_shape=jax.ShapeDtypeStruct((512, 128), F32),
        in_specs=[hbm] * 9,
        out_specs=vm,
        scratch_shapes=[
            pltpu.VMEM((2, 2, 8, 16, 128), BF16),
            pltpu.VMEM((2, 256), jnp.int32),
            pltpu.VMEM((128, 256), BF16),
            pltpu.VMEM((128, 256), BF16),
            pltpu.VMEM((128, 128), BF16),
            pltpu.VMEM((128, 128), BF16),
            pltpu.VMEM((128, 512), BF16),
            pltpu.VMEM((4, 128), BF16),
            pltpu.VMEM((128, 128), BF16),
            pltpu.VMEM((NY, 2, 16, 256), BF16),
            pltpu.VMEM((NQ, 16, 256), BF16),
            pltpu.VMEM((NY, 16, 128), BF16),
            pltpu.VMEM((NY, 2, 16, 256), BF16),
            pltpu.VMEM((NQ, 16, 256), BF16),
            pltpu.VMEM((NY, 2, 2, 16, 128), BF16),
            pltpu.VMEM((NY, 16, 128), BF16),
            pltpu.VMEM((NQ, 16, 256), BF16),
            pltpu.VMEM((NY, 32, 256), BF16),
            pltpu.VMEM((NQ, 4, 16, 128), BF16),
            pltpu.VMEM((NQ, 16, 256), BF16),
            pltpu.VMEM((NY, 32, 256), BF16),
            pltpu.VMEM((NQ, 4, 16, 128), BF16),
            pltpu.VMEM((NY, 32, 256), BF16),
            pltpu.VMEM((NY, 32, 256), BF16),
            pltpu.VMEM((NQ, 16, 256), BF16),
            pltpu.VMEM((NQ, 16, 256), BF16),
            pltpu.VMEM((16, 128), BF16),
            pltpu.VMEM((NY, 16, 128), BF16),
            pltpu.VMEM((8, 16, 128), BF16),
            pltpu.VMEM((NQ, 8, 16, 128), BF16),
            pltpu.VMEM((2, 4, 256, 256), F32),
            pltpu.SemaphoreType.DMA((18,)),
            pltpu.SemaphoreType.DMA((18,)),
            pltpu.SemaphoreType.DMA((9,)),
        ],
        compiler_params=pltpu.CompilerParams(
            collective_id=0, has_side_effects=True, vmem_limit_bytes=60 * 1024 * 1024
        ),
    )(pair.reshape(2, 2, 8, 16, 128), pair_mask, wl, wr, wg, wo, wa, wb.T, wao)
    return out.reshape(256, 2, 128)


def solution(mesh):
    rows = ("dp", "dap")
    return jax.shard_map(
        shards,
        mesh=mesh,
        in_specs=(P(rows, None, None), P(rows, None), P(), P(), P(), P(), P(), P(), P()),
        out_specs=P("dp", "dap", None),
        check_vma=False,
    )
```

time: 57.6 us -> 50.4 us (0.88)
  local copies, waits for them, and re-layouts: 6.52 us -> 1.67 us
  Pallas kernels: 50.6 us -> 48.6 us
    unnamed x18 -> x1, local copies, waits for them, and re-layouts: 6.52 us -> 1.67 us
    pallas_call x1, Pallas kernels: 50.6 us -> 48.6 us  [shards(): pl.pallas_call(kernel, out_shape=jax.ShapeDtypeStruct((512, 128), F32), i...]
where the time goes in v2:
time: 50.4 us; the launch traced here: 50.3 us
  Pallas kernels  48.6 us (96%)
  local copies, waits for them, and re-layouts  1.67 us (3%)
    pallas_call x1, Pallas kernels, shards(): pl.pallas_call(kernel, out_shape=jax.ShapeDtypeStruct((512, 128), F32), i...  48.6 us
    unnamed x1, local copies, waits for them, and re-layouts  1.67 us

profile of v2, /device:TPU:1, one launch (start us, length us, event | category | flops | bytes accessed | tf_op | source)
XLA Modules:
  0.0 50.3 jit_solution(7753222114840779980)
XLA Ops:
  0.0 48.6 %shard_map.91 = f32[512,128]{1,0:T(8,128)} custom-call(bf16[2,2,8,16,128]{4,3,2,1,0:T(8,128)(2,1)} %bitcast.4, s32[2,256]{1,0:T(2,128)} %mask_in.1, bf16[128,256]{1,0:T(8,128)(2,1)} %wl_in.1, bf16[128,256]{1,0:T(8,128)(2,1)} %wr_in.1, bf16[128,128]{1,0:T(8,128)(2,1)} %wg_in.1, bf16[128,128]{1,0:T(8,128)(2,1)} %wo_in.1, bf16[128,512]{1,0:T(8,128)(2,1)} %wa_in.1, ...), custom_call_target="tpu_custom_call" | custom-call | tf_op jit(solution)/shard_map/pallas_call | solution.py:281
  48.6 1.7 %copy.11 = f32[256,2,128]{2,1,0:T(2,128)} copy(f32[256,2,128]{2,1,0:T(2,128)} %bitcast.3) | data formatting | bytes 524288

commit v3 on v2

--- a/solution.py
+++ b/solution.py
@@ -1,4 +1,4 @@
-import functools
+import itertools
 
 import jax
 import jax.numpy as jnp
@@ -19,7 +19,12 @@
 
 FAR_Y = (4, 3, 5, 2, 6, 1, 7)
 FAR_Q = tuple((dz, dx, dc) for dz, dx in ((1, 2), (1, 1), (1, 3), (0, 2), (0, 1), (0, 3), (1, 0)) for dc in (0, 1)) + ((0, 0, 1),)
-FAR_CHIP = tuple(step for step in FAR_Q if step[2] == 0)
+FAR_ALL = tuple(
+    sorted(
+        (s for s in itertools.product(range(2), range(8), range(4), range(2)) if any(s)),
+        key=lambda s: -(s[0] + min(s[1], 8 - s[1]) + min(s[2], 4 - s[2]) + 0.1 * s[3]),
+    )
+)
 
 
 def device_of(q, y):
@@ -58,8 +63,7 @@
     pair_ref, mask_ref, wl_ref, wr_ref, wg_ref, wo_ref, wa_ref, wb_ref, wao_ref,
     send_l, send_r, send_m, got_l, got_r, got_p, got_m,
     next_l, next_r, next_p, have_l, have_r, have_p,
-    send_t, got_t, next_t, have_t,
-    send_b, got_b, next_b, have_b, scores, ssem, rsem, lsem,
+    send_t, have_t, send_b, have_b, scores, ssem, rsem, lsem,
 ):
     me = lax.axis_index("dap")
     zl, y, xc = me // 64, (me // 8) % 8, me % 8
@@ -81,6 +85,7 @@
         pl.semaphore_signal(barrier, inc=1, device_id={"dap": peer}, device_id_type=MESH)
 
     sent, due = {}, {}
+    near = moved(q, (0, 0, 1))
 
     def send(src, dst, k, peer):
         pltpu.make_async_remote_copy(
@@ -115,7 +120,6 @@
 
     lane, col = grid_of(128, 128)
     by_q = onehot((lane % 16 == col // 8) & (lane // 16 == col % 8))
-    q_by = onehot((col % 16 == lane // 8) & (col // 16 == lane % 8))
 
     def edge(w):
         both = mm(w, zn, TT)
@@ -138,10 +142,13 @@
 
     r, s = grid_of(256, 256)
     turn = onehot((r // 16 == s % 16) & ((r // 8) % 2 == (s // 16) % 2) & (r % 8 == s // 32))
-    back = onehot((s // 16 == r % 16) & ((s // 8) % 2 == (r // 16) % 2) & (s % 8 == r // 32))
+    split = onehot((r % 2 == (s // 8) % 2) & ((r // 2) % 16 == s // 16) & (r // 32 == s % 8))
+    twice = onehot(lax.broadcasted_iota(jnp.int32, (512, 256), 0) // 2 == lax.broadcasted_iota(jnp.int32, (512, 256), 1))
+    even = lax.broadcasted_iota(jnp.int32, (512, 128), 0) % 2 == 0
+    gather = onehot((s % 4 == r // 64) & (s // 4 == r % 64))
 
     arrive(1)
-    next_r[...] = mm(back, got_r[...].reshape(256, 256)).astype(BF16).reshape(NY, 32, 256)
+    next_r[...] = mm(split, got_r[...].reshape(256, 256)).astype(BF16).reshape(NY, 32, 256)
     send_y(lambda to: next_r.at[to], have_r, 5)
     arrive(0)
     next_l[...] = mm(turn, got_l[...].reshape(256, 256)).astype(BF16).reshape(NQ, 16, 256)
@@ -160,11 +167,17 @@
     got_m[y] = send_m[y]
 
     arrive(5)
+    doubled = mm(twice, have_r[...].reshape(256, 256)).astype(BF16)
     arrive(4)
-    tri = mm(have_r[...].reshape(256, 256), have_l[...].reshape(256, 256), NT)
-    send_t[...] = tri.astype(BF16).reshape(NY, 32, 256)
-    send_y(lambda to: send_t.at[to], got_t, 7)
-    got_t[y] = send_t[y]
+    tri = mm(doubled, have_l[...].reshape(256, 256), NT)
+    tri = jnp.where(even, tri[:, :128], tri[:, 128:])
+    send_t[...] = tri.reshape(128, 4, 128).astype(BF16)
+    sent[7] = due[7] = have_t.at[pl.ds(0, 127)]
+    place = y * 16 + q
+    for step in FAR_ALL:
+        to, there = moved(q, (step[0], step[2], step[3])), (y + step[1]) % NY
+        send(send_t.at[there * 16 + to], have_t.at[place], 7, device_of(to, there))
+    have_t[place] = send_t[place]
 
     arrive(2)
     arrive(3)
@@ -192,33 +205,37 @@
     wk = wa[:, 128:256]
     wq_t, wv_t, wgate_t = wa[:, :128], wa[:, 256:384], wa[:, 384:]
 
+    order = onehot(
+        (s // 128 == (r // 16) % 2)
+        & ((s // 16) % 8 == r % 8)
+        & ((s // 8) % 2 == r // 128)
+        & ((s // 4) % 2 == (r // 8) % 2)
+        & (s % 4 == (r // 32) % 4)
+    )
     arrive(7)
-    next_t[...] = mm(turn, got_t[...].reshape(256, 256)).astype(BF16).reshape(NQ, 16, 256)
-    send_q(lambda to: next_t.at[to], have_t, 8)
-    have_t[q] = next_t[q]
-    wo = mm(q_by, wo_ref[...]).astype(BF16)
-    order = onehot(
-        (col // 16 == lane % 8)
-        & ((col // 8) % 2 == lane // 64)
-        & ((col // 4) % 2 == (lane // 8) % 2)
-        & (col % 4 == (lane // 16) % 4)
-    )
-    arrive(8)
 
     pair1, yns = [], []
-    tris = have_t[...].astype(F32).reshape(NQ, 2, 8, 256)
-    for jj in range(2):
-        t = tris[:, jj].reshape(128, 256)
+    tris = [mm(gather, have_t[b * 64 : b * 64 + 64].reshape(256, 128)).reshape(4, 64, 128) for b in range(2)]
+    for jj in range(2):
+        t = jnp.concatenate(
+            [jnp.concatenate([tris[b][jj * 2 + half] for b in range(2)], axis=0) for half in range(2)], axis=1
+        )
         tn = norm(t, 0).astype(BF16)
-        p1 = pairs[jj] + gates[jj] * mm(tn, wo, YN)
+        p1 = pairs[jj] + gates[jj] * mm(tn, wo_ref[...], YN)
         pair1.append(p1)
         yns.append(norm(p1, 1).astype(BF16))
 
     parts = [mm(wb_ref[...], yn, NT) for yn in yns]
     both = jnp.concatenate(parts, axis=0)
     send_b[...] = jnp.concatenate([both[:, :128], both[:, 128:]], axis=0).astype(BF16)
-    send_y(lambda to: send_b, got_b, 9)
-    got_b[y] = send_b[...]
+    chip, core = q // 2, q % 2
+    for step in FAR_ALL:
+        if step[3] == 0:
+            to, there = moved(q, (step[0], step[2], 0)), (y + step[1]) % NY
+            send(send_b, have_b.at[chip, core, y], 9 + step[1], device_of(to, there))
+    have_b[chip, core, y] = send_b[...]
+    for k in range(NY):
+        sent[9 + k] = have_b.at[pl.ds(0, 8 if k else 7), 0, 0]
 
     keys, queries, values, out_gates = [], [], [], []
     for jj in range(2):
@@ -227,17 +244,6 @@
         values.append(mm(wv_t, yns[jj], TT).astype(BF16))
         out_gates.append(jax.nn.sigmoid(mm(wgate_t, yns[jj], TT)))
 
-    arrive(9)
-    next_b[...] = mm(order, got_b[...].reshape(128, 128)).astype(BF16).reshape(8, 16, 128)
-    near = moved(q, (0, 0, 1))
-    for k, step in enumerate(FAR_CHIP):
-        sent[10 + k] = have_b.at[0]
-        to = moved(q, step)
-        send(next_b, have_b.at[q], 10 + k, device_of(to, y))
-    have_b[q] = next_b[...]
-    sent[17] = due[17] = have_b.at[pl.ds(0, 8)]
-    send(next_b, have_b.at[q], 17, device_of(near, y))
-
     head_row = lax.broadcasted_iota(jnp.int32, (128, 256), 0) // 32
     scale = F32(32.0**-0.5)
     for jj in range(2):
@@ -245,16 +251,17 @@
             qh = jnp.where(head_row == h, queries[jj].astype(F32), F32(0)).astype(BF16)
             scores[jj, h] = mm(keys[jj], qh) * scale
 
-    for k in reversed(range(7)):
-        dz, dx, _ = FAR_CHIP[k]
-        at = moved(q, (dz, -dx, 0))
-        wait_on(have_b.at[0], rsem.at[10 + k])
-        send(have_b.at[at], have_b.at[at], 17, device_of(near, y))
+    sent[17] = due[17] = have_b.at[:, 0]
+    for k in (0, 1, 7, 2, 6, 3, 5, 4):
+        wait_on(sent[9 + k], rsem.at[9 + k])
+        block = have_b.at[:, core, (y + NY - k) % NY]
+        send(block, block, 17, device_of(near, y))
     arrive(17)
+    biases = [mm(order, have_b[b].reshape(256, 128)).astype(BF16).reshape(8, 32, 128) for b in range(8)]
     atts = [[], []]
     for h in range(4):
         bias = jnp.concatenate(
-            [mm(eye, have_b[:, kh * 4 + h].reshape(256, 128), NT) for kh in range(2)], axis=0
+            [mm(eye, jnp.concatenate([b[kh * 4 + h] for b in biases], axis=0), NT) for kh in range(2)], axis=0
         )
         for jj in range(2):
             live = jnp.concatenate([lives[jj], lives[jj]], axis=1) > 0.5
@@ -306,14 +313,10 @@
             pltpu.VMEM((NQ, 16, 256), BF16),
             pltpu.VMEM((NY, 32, 256), BF16),
             pltpu.VMEM((NQ, 4, 16, 128), BF16),
-            pltpu.VMEM((NY, 32, 256), BF16),
-            pltpu.VMEM((NY, 32, 256), BF16),
-            pltpu.VMEM((NQ, 16, 256), BF16),
-            pltpu.VMEM((NQ, 16, 256), BF16),
+            pltpu.VMEM((128, 4, 128), BF16),
+            pltpu.VMEM((128, 4, 128), BF16),
             pltpu.VMEM((16, 128), BF16),
-            pltpu.VMEM((NY, 16, 128), BF16),
-            pltpu.VMEM((8, 16, 128), BF16),
-            pltpu.VMEM((NQ, 8, 16, 128), BF16),
+            pltpu.VMEM((8, 2, NY, 16, 128), BF16),
             pltpu.VMEM((2, 4, 256, 256), F32),
             pltpu.SemaphoreType.DMA((18,)),
             pltpu.SemaphoreType.DMA((18,)),

time: 50.4 us -> 46.3 us (0.919)
  Pallas kernels: 48.6 us -> 44.5 us
    pallas_call x1, Pallas kernels: 48.6 us -> 44.5 us  [shards(): pl.pallas_call(kernel, out_shape=jax.ShapeDtypeStruct((512, 128), F32), i...]
where the time goes in v3:
time: 46.3 us; the launch traced here: 46.2 us
  Pallas kernels  44.5 us (96%)
  local copies, waits for them, and re-layouts  1.67 us (4%)
    pallas_call x1, Pallas kernels, shards(): pl.pallas_call(kernel, out_shape=jax.ShapeDtypeStruct((512, 128), F32), i...  44.5 us
    unnamed x1, local copies, waits for them, and re-layouts  1.67 us

profile of v3, /device:TPU:1, one launch (start us, length us, event | category | flops | bytes accessed | tf_op | source)
XLA Modules:
  0.0 46.2 jit_solution(6257423207328210250)
XLA Ops:
  0.0 44.5 %shard_map.91 = f32[512,128]{1,0:T(8,128)} custom-call(bf16[2,2,8,16,128]{4,3,2,1,0:T(8,128)(2,1)} %bitcast.4, s32[2,256]{1,0:T(2,128)} %mask_in.1, bf16[128,256]{1,0:T(8,128)(2,1)} %wl_in.1, bf16[128,256]{1,0:T(8,128)(2,1)} %wr_in.1, bf16[128,128]{1,0:T(8,128)(2,1)} %wg_in.1, bf16[128,128]{1,0:T(8,128)(2,1)} %wo_in.1, bf16[128,512]{1,0:T(8,128)(2,1)} %wa_in.1, ...), custom_call_target="tpu_custom_call" | custom-call | tf_op jit(solution)/shard_map/pallas_call | solution.py:288
  44.5 1.7 %copy.11 = f32[256,2,128]{2,1,0:T(2,128)} copy(f32[256,2,128]{2,1,0:T(2,128)} %bitcast.3) | data formatting | bytes 524288

commit v4 on v3

--- a/solution.py
+++ b/solution.py
@@ -140,22 +140,6 @@
     got_l[y] = send_l[y]
     got_r[q] = send_r[q]
 
-    r, s = grid_of(256, 256)
-    turn = onehot((r // 16 == s % 16) & ((r // 8) % 2 == (s // 16) % 2) & (r % 8 == s // 32))
-    split = onehot((r % 2 == (s // 8) % 2) & ((r // 2) % 16 == s // 16) & (r // 32 == s % 8))
-    twice = onehot(lax.broadcasted_iota(jnp.int32, (512, 256), 0) // 2 == lax.broadcasted_iota(jnp.int32, (512, 256), 1))
-    even = lax.broadcasted_iota(jnp.int32, (512, 128), 0) % 2 == 0
-    gather = onehot((s % 4 == r // 64) & (s // 4 == r % 64))
-
-    arrive(1)
-    next_r[...] = mm(split, got_r[...].reshape(256, 256)).astype(BF16).reshape(NY, 32, 256)
-    send_y(lambda to: next_r.at[to], have_r, 5)
-    arrive(0)
-    next_l[...] = mm(turn, got_l[...].reshape(256, 256)).astype(BF16).reshape(NQ, 16, 256)
-    send_q(lambda to: next_l.at[to], have_l, 4)
-    have_l[q] = next_l[q]
-    have_r[y] = next_r[y]
-
     rows0 = jnp.where(lane % 2 == 0, maskf[0:1, :128], maskf[0:1, 128:])
     rows1 = jnp.where(lane % 2 == 0, maskf[1:2, :128], maskf[1:2, 128:])
     eye = onehot(lane == col)
@@ -165,6 +149,22 @@
     send_y(lambda to: send_m.at[to], got_m, 3)
     got_p[y] = pair_ref[:, :, y]
     got_m[y] = send_m[y]
+
+    r, s = grid_of(256, 256)
+    turn = onehot((r // 16 == s % 16) & ((r // 8) % 2 == (s // 16) % 2) & (r % 8 == s // 32))
+    split = onehot((r % 2 == (s // 8) % 2) & ((r // 2) % 16 == s // 16) & (r // 32 == s % 8))
+    twice = onehot(lax.broadcasted_iota(jnp.int32, (512, 256), 0) // 2 == lax.broadcasted_iota(jnp.int32, (512, 256), 1))
+    even = lax.broadcasted_iota(jnp.int32, (512, 128), 0) % 2 == 0
+    gather = onehot((s % 4 == r // 64) & (s // 4 == r % 64))
+
+    arrive(1)
+    next_r[...] = mm(split, got_r[...].reshape(256, 256)).astype(BF16).reshape(NY, 32, 256)
+    send_y(lambda to: next_r.at[to], have_r, 5)
+    arrive(0)
+    next_l[...] = mm(turn, got_l[...].reshape(256, 256)).astype(BF16).reshape(NQ, 16, 256)
+    send_q(lambda to: next_l.at[to], have_l, 4)
+    have_l[q] = next_l[q]
+    have_r[y] = next_r[y]
 
     arrive(5)
     doubled = mm(twice, have_r[...].reshape(256, 256)).astype(BF16)
@@ -285,6 +285,7 @@
 def shards(pair, pair_mask, wl, wr, wg, wo, wa, wb, wao):
     vm = pl.BlockSpec(memory_space=pltpu.VMEM)
     hbm = pl.BlockSpec(memory_space=pltpu.HBM)
+    inputs = (pair.reshape(2, 2, 8, 16, 128), pair_mask, wl, wr, wg, wo, wa, wb.T, wao)
     out = pl.pallas_call(
         kernel,
         out_shape=jax.ShapeDtypeStruct((512, 128), F32),
@@ -323,9 +324,9 @@
             pltpu.SemaphoreType.DMA((9,)),
         ],
         compiler_params=pltpu.CompilerParams(
-            collective_id=0, has_side_effects=True, vmem_limit_bytes=60 * 1024 * 1024
+            collective_id=0, has_side_effects=True, vmem_limit_bytes=32 * 1024 * 1024
         ),
-    )(pair.reshape(2, 2, 8, 16, 128), pair_mask, wl, wr, wg, wo, wa, wb.T, wao)
+    )(*(pltpu.with_memory_space_constraint(a, pltpu.HBM) for a in inputs))
     return out.reshape(256, 2, 128)
 
 

time: 46.3 us -> 43.6 us (0.942)
  Pallas kernels: 44.5 us -> 42.8 us
  local copies, waits for them, and re-layouts: 1.67 us -> 0.71 us
    pallas_call x1, Pallas kernels: 44.5 us -> 42.8 us  [shards(): pl.pallas_call(kernel, out_shape=jax.ShapeDtypeStruct((512, 128), F32), i...]
    unnamed x1, local copies, waits for them, and re-layouts: 1.67 us -> 0.71 us
where the time goes in v4:
time: 43.6 us; the launch traced here: 43.5 us
  Pallas kernels  42.8 us (98%)
  local copies, waits for them, and re-layouts  0.71 us (2%)
    pallas_call x1, Pallas kernels, shards(): pl.pallas_call(kernel, out_shape=jax.ShapeDtypeStruct((512, 128), F32), i...  42.8 us

profile of v4, /device:TPU:1, one launch (start us, length us, event | category | flops | bytes accessed | tf_op | source)
XLA Modules:
  0.0 43.5 jit_solution(9575272056077143732)
XLA Ops:
  0.0 42.8 %shard_map.91 = f32[512,128]{1,0:T(8,128)S(1)} custom-call(bf16[2,2,8,16,128]{4,3,2,1,0:T(8,128)(2,1)} %bitcast.4, s32[2,256]{1,0:T(2,128)} %mask_in.1, bf16[128,256]{1,0:T(8,128)(2,1)} %wl_in.1, bf16[128,256]{1,0:T(8,128)(2,1)} %wr_in.1, bf16[128,128]{1,0:T(8,128)(2,1)} %wg_in.1, bf16[128,128]{1,0:T(8,128)(2,1)} %wo_in.1, bf16[128,512]{1,0:T(8,128)(2,1)} %wa_in.1, ...), custom_call_target="tpu_custom_call" | custom-call | tf_op jit(solution)/shard_map/pallas_call | solution.py:289
  42.8 0.7 %copy.11 = f32[256,2,128]{2,1,0:T(2,128)} copy(f32[256,2,128]{2,1,0:T(2,128)S(1)} %bitcast.3) | data formatting | bytes 524288

commit v5 on v4

--- a/solution.py
+++ b/solution.py
@@ -68,6 +68,13 @@
     me = lax.axis_index("dap")
     zl, y, xc = me // 64, (me // 8) % 8, me % 8
     q = zl * 8 + xc
+    at_y = [(y + s) % NY for s in range(NY)]
+    at_q = {}
+    for dz, dx, dc in itertools.product(range(2), range(4), range(2)):
+        z, xx, cc = (zl + dz) % 2, (q // 2 + dx) % 4 * 2, (q + dc) % 2
+        at_q[dz, dx, dc] = (z * 8 + xx + cc, z * 64 + xx + cc)
+    y_part = [v * 8 for v in at_y]
+    y_slot = [v * 16 for v in at_y]
 
     loads = [
         pltpu.make_async_copy(a, b, lsem.at[k])
@@ -166,19 +173,6 @@
     have_l[q] = next_l[q]
     have_r[y] = next_r[y]
 
-    arrive(5)
-    doubled = mm(twice, have_r[...].reshape(256, 256)).astype(BF16)
-    arrive(4)
-    tri = mm(doubled, have_l[...].reshape(256, 256), NT)
-    tri = jnp.where(even, tri[:, :128], tri[:, 128:])
-    send_t[...] = tri.reshape(128, 4, 128).astype(BF16)
-    sent[7] = due[7] = have_t.at[pl.ds(0, 127)]
-    place = y * 16 + q
-    for step in FAR_ALL:
-        to, there = moved(q, (step[0], step[2], step[3])), (y + step[1]) % NY
-        send(send_t.at[there * 16 + to], have_t.at[place], 7, device_of(to, there))
-    have_t[place] = send_t[place]
-
     arrive(2)
     arrive(3)
     m0 = got_m[...].astype(F32)
@@ -192,6 +186,19 @@
     send_q(lambda to: next_p.at[to], have_p, 6)
     have_p[q] = next_p[q]
 
+    arrive(5)
+    doubled = mm(twice, have_r[...].reshape(256, 256)).astype(BF16)
+    arrive(4)
+    tri = mm(doubled, have_l[...].reshape(256, 256), NT)
+    tri = jnp.where(even, tri[:, :128], tri[:, 128:])
+    send_t[...] = tri.reshape(128, 4, 128).astype(BF16)
+    sent[7] = due[7] = have_t.at[pl.ds(0, 127)]
+    place = y * 16 + q
+    for step in FAR_ALL:
+        to, part = at_q[step[0], step[2], step[3]]
+        send(send_t.at[y_slot[step[1]] + to], have_t.at[place], 7, part + y_part[step[1]])
+    have_t[place] = send_t[place]
+
     arrive(6)
     pairs, gates, lives = [], [], []
     pick = onehot(lane == zl)
@@ -231,8 +238,7 @@
     chip, core = q // 2, q % 2
     for step in FAR_ALL:
         if step[3] == 0:
-            to, there = moved(q, (step[0], step[2], 0)), (y + step[1]) % NY
-            send(send_b, have_b.at[chip, core, y], 9 + step[1], device_of(to, there))
+            send(send_b, have_b.at[chip, core, y], 9 + step[1], at_q[step[0], step[2], 0][1] + y_part[step[1]])
     have_b[chip, core, y] = send_b[...]
     for k in range(NY):
         sent[9 + k] = have_b.at[pl.ds(0, 8 if k else 7), 0, 0]
@@ -259,6 +265,7 @@
     arrive(17)
     biases = [mm(order, have_b[b].reshape(256, 128)).astype(BF16).reshape(8, 32, 128) for b in range(8)]
     atts = [[], []]
+    ones = jnp.ones((16, 256), BF16)
     for h in range(4):
         bias = jnp.concatenate(
             [mm(eye, jnp.concatenate([b[kh * 4 + h] for b in biases], axis=0), NT) for kh in range(2)], axis=0
@@ -267,9 +274,8 @@
             live = jnp.concatenate([lives[jj], lives[jj]], axis=1) > 0.5
             sc = jnp.where(live, scores[jj, h] + bias, F32(-1e9))
             e = jnp.exp(sc - jnp.max(sc, axis=0, keepdims=True))
-            w = (e / jnp.sum(e, axis=0, keepdims=True)).astype(BF16)
-            o = mm(values[jj][h * 32 : (h + 1) * 32], w)
-            atts[jj].append(out_gates[jj][h * 32 : (h + 1) * 32] * o)
+            o = mm(jnp.concatenate([values[jj][h * 32 : (h + 1) * 32], ones], axis=0), e.astype(BF16))
+            atts[jj].append(out_gates[jj][h * 32 : (h + 1) * 32] * (o[:32] / o[32:33]))
     for jj in range(2):
         att = jnp.concatenate(atts[jj], axis=0).astype(BF16)
         res = pair1[jj] + mm(att, wao_ref[...], YN)

time: 43.6 us -> 42.7 us (0.979)
  Pallas kernels: 42.8 us -> 41.9 us
    pallas_call x1, Pallas kernels: 42.8 us -> 41.9 us  [shards(): pl.pallas_call(kernel, out_shape=jax.ShapeDtypeStruct((512, 128), F32), i...]
where the time goes in v5:
time: 42.7 us; the launch traced here: 42.6 us
  Pallas kernels  41.9 us (98%)
  local copies, waits for them, and re-layouts  0.71 us (2%)
    pallas_call x1, Pallas kernels, shards(): pl.pallas_call(kernel, out_shape=jax.ShapeDtypeStruct((512, 128), F32), i...  41.9 us

profile of v5, /device:TPU:1, one launch (start us, length us, event | category | flops | bytes accessed | tf_op | source)
XLA Modules:
  0.0 42.6 jit_solution(8741149684829556773)
XLA Ops:
  0.0 41.9 %shard_map.91 = f32[512,128]{1,0:T(8,128)S(1)} custom-call(bf16[2,2,8,16,128]{4,3,2,1,0:T(8,128)(2,1)} %bitcast.4, s32[2,256]{1,0:T(2,128)} %mask_in.1, bf16[128,256]{1,0:T(8,128)(2,1)} %wl_in.1, bf16[128,256]{1,0:T(8,128)(2,1)} %wr_in.1, bf16[128,128]{1,0:T(8,128)(2,1)} %wg_in.1, bf16[128,128]{1,0:T(8,128)(2,1)} %wo_in.1, bf16[128,512]{1,0:T(8,128)(2,1)} %wa_in.1, ...), custom_call_target="tpu_custom_call" | custom-call | tf_op jit(solution)/shard_map/pallas_call | solution.py:295
  41.9 0.7 %copy.11 = f32[256,2,128]{2,1,0:T(2,128)} copy(f32[256,2,128]{2,1,0:T(2,128)S(1)} %bitcast.3) | data formatting | bytes 524288

commit v6 on v5

--- a/solution.py
+++ b/solution.py
@@ -27,13 +27,8 @@
 )
 
 
-def device_of(q, y):
-    return (q // 8) * 64 + y * 8 + q % 8
-
-
-def moved(q, step):
-    dz, dx, dc = step
-    return ((q // 8 + dz) % 2) * 8 + ((q // 2 + dx) % 4) * 2 + (q + dc) % 2
+def natural(q):
+    return (q // 4) % 2 * 8 + q % 4 * 2 + q // 8
 
 
 def mm(a, b, dims=(((1,), (0,)), ((), ()))):
@@ -63,16 +58,16 @@
     pair_ref, mask_ref, wl_ref, wr_ref, wg_ref, wo_ref, wa_ref, wb_ref, wao_ref,
     send_l, send_r, send_m, got_l, got_r, got_p, got_m,
     next_l, next_r, next_p, have_l, have_r, have_p,
-    send_t, have_t, send_b, have_b, scores, ssem, rsem, lsem,
+    send_t, have_t, send_b, have_b, scores, pair1, out_gates, ssem, rsem, lsem,
 ):
     me = lax.axis_index("dap")
-    zl, y, xc = me // 64, (me // 8) % 8, me % 8
-    q = zl * 8 + xc
+    zl, y, x_at, core = me // 64, (me // 8) % 8, (me // 2) % 4, me % 2
+    q = core * 8 + zl * 4 + x_at
     at_y = [(y + s) % NY for s in range(NY)]
     at_q = {}
     for dz, dx, dc in itertools.product(range(2), range(4), range(2)):
-        z, xx, cc = (zl + dz) % 2, (q // 2 + dx) % 4 * 2, (q + dc) % 2
-        at_q[dz, dx, dc] = (z * 8 + xx + cc, z * 64 + xx + cc)
+        z, xx, cc = (zl + dz) % 2, (x_at + dx) % 4, (core + dc) % 2
+        at_q[dz, dx, dc] = (cc * 8 + z * 4 + xx, z * 64 + xx * 2 + cc)
     y_part = [v * 8 for v in at_y]
     y_slot = [v * 16 for v in at_y]
 
@@ -87,12 +82,13 @@
         load.start()
     barrier = pltpu.get_barrier_semaphore()
 
-    peers = [device_of(q, (y + s) % NY) for s in FAR_Y] + [device_of(moved(q, step), y) for step in FAR_Q]
+    own = at_q[0, 0, 0][1]
+    peers = [own + y_part[s] for s in FAR_Y] + [at_q[step][1] + y_part[0] for step in FAR_Q]
     for peer in peers:
         pl.semaphore_signal(barrier, inc=1, device_id={"dap": peer}, device_id_type=MESH)
 
     sent, due = {}, {}
-    near = moved(q, (0, 0, 1))
+    near = at_q[0, 0, 1][1] + y_part[0]
 
     def send(src, dst, k, peer):
         pltpu.make_async_remote_copy(
@@ -103,14 +99,13 @@
     def send_y(src, dst, k):
         sent[k] = due[k] = dst.at[pl.ds(0, NY - 1)]
         for s in FAR_Y:
-            to = (y + s) % NY
-            send(src(to), dst.at[y], k, device_of(q, to))
+            send(src(at_y[s]), dst.at[y], k, own + y_part[s])
 
     def send_q(src, dst, k):
         sent[k] = due[k] = dst.at[pl.ds(0, NQ - 1)]
         for step in FAR_Q:
-            to = moved(q, step)
-            send(src(to), dst.at[q], k, device_of(to, y))
+            to, part = at_q[step]
+            send(src(to), dst.at[q], k, part + y_part[0])
 
     def wait_on(ref, sem):
         pltpu.make_async_copy(ref, ref, sem).wait()
@@ -183,8 +178,8 @@
         part = mm(turn, got_p[:, :, z].reshape(256, 128)).astype(BF16)
         next_p[z * 8 : z * 8 + 8, 0:2] = part.reshape(8, 2, 16, 128)
         next_p[z * 8 : z * 8 + 8, 2:4] = m01
-    send_q(lambda to: next_p.at[to], have_p, 6)
-    have_p[q] = next_p[q]
+    send_q(lambda to: next_p.at[natural(to)], have_p, 6)
+    have_p[q] = next_p[natural(q)]
 
     arrive(5)
     doubled = mm(twice, have_r[...].reshape(256, 256)).astype(BF16)
@@ -221,7 +216,7 @@
     )
     arrive(7)
 
-    pair1, yns = [], []
+    yns = []
     tris = [mm(gather, have_t[b * 64 : b * 64 + 64].reshape(256, 128)).reshape(4, 64, 128) for b in range(2)]
     for jj in range(2):
         t = jnp.concatenate(
@@ -229,60 +224,71 @@
         )
         tn = norm(t, 0).astype(BF16)
         p1 = pairs[jj] + gates[jj] * mm(tn, wo_ref[...], YN)
-        pair1.append(p1)
+        pair1[jj] = p1.reshape(2, 128, 128)
         yns.append(norm(p1, 1).astype(BF16))
 
     parts = [mm(wb_ref[...], yn, NT) for yn in yns]
     both = jnp.concatenate(parts, axis=0)
     send_b[...] = jnp.concatenate([both[:, :128], both[:, 128:]], axis=0).astype(BF16)
-    chip, core = q // 2, q % 2
+    chip = q % 8
     for step in FAR_ALL:
         if step[3] == 0:
-            send(send_b, have_b.at[chip, core, y], 9 + step[1], at_q[step[0], step[2], 0][1] + y_part[step[1]])
-    have_b[chip, core, y] = send_b[...]
+            send(send_b, have_b.at[core, chip, y], 9 + step[1], at_q[step[0], step[2], 0][1] + y_part[step[1]])
+    have_b[core, chip, y] = send_b[...]
     for k in range(NY):
-        sent[9 + k] = have_b.at[pl.ds(0, 8 if k else 7), 0, 0]
-
-    keys, queries, values, out_gates = [], [], [], []
+        sent[9 + k] = have_b.at[0, pl.ds(0, 8 if k else 7), 0]
+
+    keys, queries, values = [], [], []
     for jj in range(2):
         keys.append(mm(yns[jj], wk).astype(BF16))
         queries.append(mm(wq_t, yns[jj], TT).astype(BF16))
         values.append(mm(wv_t, yns[jj], TT).astype(BF16))
-        out_gates.append(jax.nn.sigmoid(mm(wgate_t, yns[jj], TT)))
+        gate = jax.nn.sigmoid(mm(wgate_t, yns[jj], TT))
+        for half in range(2):
+            out_gates[jj, half] = gate[:, half * 128 : half * 128 + 128]
 
     head_row = lax.broadcasted_iota(jnp.int32, (128, 256), 0) // 32
     scale = F32(32.0**-0.5)
     for jj in range(2):
         for h in range(4):
             qh = jnp.where(head_row == h, queries[jj].astype(F32), F32(0)).astype(BF16)
-            scores[jj, h] = mm(keys[jj], qh) * scale
-
-    sent[17] = due[17] = have_b.at[:, 0]
+            score = mm(keys[jj], qh) * scale
+            for half in range(2):
+                scores[jj, h, half] = score[:, half * 128 : half * 128 + 128]
+
+    sent[17] = due[17] = have_b.at[0]
     for k in (0, 1, 7, 2, 6, 3, 5, 4):
         wait_on(sent[9 + k], rsem.at[9 + k])
-        block = have_b.at[:, core, (y + NY - k) % NY]
-        send(block, block, 17, device_of(near, y))
+        block = have_b.at[core, :, (y + NY - k) % NY]
+        send(block, block, 17, near)
+
+    ones = jnp.ones((16, 256), BF16)
+
+    def finish(half):
+        biases = [
+            mm(order, have_b[half, 2 * b : 2 * b + 2].reshape(256, 128)).astype(BF16).reshape(8, 32, 128) for b in range(4)
+        ]
+        atts = [[], []]
+        for h in range(4):
+            bias = jnp.concatenate(
+                [mm(eye, jnp.concatenate([b[kh * 4 + h] for b in biases], axis=0), NT) for kh in range(2)], axis=0
+            )
+            for jj in range(2):
+                sc = jnp.where(lives[jj] > 0.5, scores[jj, h, half] + bias, F32(-1e9))
+                e = jnp.exp(sc - jnp.max(sc, axis=0, keepdims=True))
+                o = mm(jnp.concatenate([values[jj][h * 32 : (h + 1) * 32], ones], axis=0), e.astype(BF16))
+                atts[jj].append(o[:32] / o[32:33])
+        for jj in range(2):
+            att = (jnp.concatenate(atts[jj], axis=0) * out_gates[jj, half]).astype(BF16)
+            res = pair1[jj, half] + mm(att, wao_ref[...], YN)
+            for k in range(8):
+                for ii in range(2):
+                    start = (k // 4) * 256 + (k % 4 * 2 + half) * 4 + ii * 2 + jj
+                    out_ref[pl.ds(start, 8, stride=32), :] = res[k * 16 + ii * 8 : k * 16 + ii * 8 + 8]
+
+    finish(core)
     arrive(17)
-    biases = [mm(order, have_b[b].reshape(256, 128)).astype(BF16).reshape(8, 32, 128) for b in range(8)]
-    atts = [[], []]
-    ones = jnp.ones((16, 256), BF16)
-    for h in range(4):
-        bias = jnp.concatenate(
-            [mm(eye, jnp.concatenate([b[kh * 4 + h] for b in biases], axis=0), NT) for kh in range(2)], axis=0
-        )
-        for jj in range(2):
-            live = jnp.concatenate([lives[jj], lives[jj]], axis=1) > 0.5
-            sc = jnp.where(live, scores[jj, h] + bias, F32(-1e9))
-            e = jnp.exp(sc - jnp.max(sc, axis=0, keepdims=True))
-            o = mm(jnp.concatenate([values[jj][h * 32 : (h + 1) * 32], ones], axis=0), e.astype(BF16))
-            atts[jj].append(out_gates[jj][h * 32 : (h + 1) * 32] * (o[:32] / o[32:33]))
-    for jj in range(2):
-        att = jnp.concatenate(atts[jj], axis=0).astype(BF16)
-        res = pair1[jj] + mm(att, wao_ref[...], YN)
-        for qq in range(NQ):
-            for ii in range(2):
-                start = (qq // 8) * 256 + (qq % 8) * 4 + ii * 2 + jj
-                out_ref[pl.ds(start, 8, stride=32), :] = res[qq * 16 + ii * 8 : qq * 16 + ii * 8 + 8]
+    finish(1 - core)
 
     for k, ref in sent.items():
         wait_on(ref, ssem.at[k])
@@ -323,8 +329,10 @@
             pltpu.VMEM((128, 4, 128), BF16),
             pltpu.VMEM((128, 4, 128), BF16),
             pltpu.VMEM((16, 128), BF16),
-            pltpu.VMEM((8, 2, NY, 16, 128), BF16),
-            pltpu.VMEM((2, 4, 256, 256), F32),
+            pltpu.VMEM((2, 8, NY, 16, 128), BF16),
+            pltpu.VMEM((2, 4, 2, 256, 128), F32),
+            pltpu.VMEM((2, 2, 128, 128), F32),
+            pltpu.VMEM((2, 2, 128, 128), F32),
             pltpu.SemaphoreType.DMA((18,)),
             pltpu.SemaphoreType.DMA((18,)),
             pltpu.SemaphoreType.DMA((9,)),

time: 42.7 us -> 42.2 us (0.988)
  Pallas kernels: 41.9 us -> 41.4 us
    pallas_call x1, Pallas kernels: 41.9 us -> 41.4 us  [shards(): pl.pallas_call(kernel, out_shape=jax.ShapeDtypeStruct((512, 128), F32), i...]
where the time goes in v6:
time: 42.2 us; the launch traced here: 42.1 us
  Pallas kernels  41.4 us (98%)
  local copies, waits for them, and re-layouts  0.71 us (2%)
    pallas_call x1, Pallas kernels, shards(): pl.pallas_call(kernel, out_shape=jax.ShapeDtypeStruct((512, 128), F32), i...  41.4 us

profile of v6, /device:TPU:1, one launch (start us, length us, event | category | flops | bytes accessed | tf_op | source)
XLA Modules:
  0.0 42.1 jit_solution(6579557297118975281)
XLA Ops:
  0.0 41.4 %shard_map.91 = f32[512,128]{1,0:T(8,128)S(1)} custom-call(bf16[2,2,8,16,128]{4,3,2,1,0:T(8,128)(2,1)} %bitcast.4, s32[2,256]{1,0:T(2,128)} %mask_in.1, bf16[128,256]{1,0:T(8,128)(2,1)} %wl_in.1, bf16[128,256]{1,0:T(8,128)(2,1)} %wr_in.1, bf16[128,128]{1,0:T(8,128)(2,1)} %wg_in.1, bf16[128,128]{1,0:T(8,128)(2,1)} %wo_in.1, bf16[128,512]{1,0:T(8,128)(2,1)} %wa_in.1, ...), custom_call_target="tpu_custom_call" | custom-call | tf_op jit(solution)/shard_map/pallas_call | solution.py:301
  41.4 0.7 %copy.11 = f32[256,2,128]{2,1,0:T(2,128)} copy(f32[256,2,128]{2,1,0:T(2,128)S(1)} %bitcast.3) | data formatting | bytes 524288

commit v7 on v6

--- a/solution.py
+++ b/solution.py
@@ -198,14 +198,15 @@
     pairs, gates, lives = [], [], []
     pick = onehot(lane == zl)
     for jj in range(2):
-        p = have_p[:, jj].reshape(256, 128).astype(F32)
-        zc = norm(p, 1).astype(BF16)
+        p = mm(eye, have_p[:, jj].reshape(256, 128), NT)
+        zc = norm(p, 0).astype(BF16)
         pairs.append(p)
-        gates.append(jax.nn.sigmoid(mm(zc, wg_ref[...])))
+        gates.append(jax.nn.sigmoid(mm(wg_ref[...], zc, YN)))
         lives.append(mm(have_p[:, 2 + jj].reshape(256, 128), pick))
     wa = wa_ref[...]
-    wk = wa[:, 128:256]
-    wq_t, wv_t, wgate_t = wa[:, :128], wa[:, 256:384], wa[:, 384:]
+    wq_t, wk_t, wv_t, wgate_t, wo_t = (
+        mm(eye, w, NT).astype(BF16) for w in (wa[:, :128], wa[:, 128:256], wa[:, 256:384], wa[:, 384:], wo_ref[...])
+    )
 
     order = onehot(
         (s // 128 == (r // 16) % 2)
@@ -216,18 +217,18 @@
     )
     arrive(7)
 
-    yns = []
+    p1s, yns = [], []
     tris = [mm(gather, have_t[b * 64 : b * 64 + 64].reshape(256, 128)).reshape(4, 64, 128) for b in range(2)]
     for jj in range(2):
         t = jnp.concatenate(
             [jnp.concatenate([tris[b][jj * 2 + half] for b in range(2)], axis=0) for half in range(2)], axis=1
         )
         tn = norm(t, 0).astype(BF16)
-        p1 = pairs[jj] + gates[jj] * mm(tn, wo_ref[...], YN)
-        pair1[jj] = p1.reshape(2, 128, 128)
-        yns.append(norm(p1, 1).astype(BF16))
-
-    parts = [mm(wb_ref[...], yn, NT) for yn in yns]
+        p1 = pairs[jj] + gates[jj] * mm(wo_t, tn)
+        p1s.append(p1)
+        yns.append(norm(p1, 0).astype(BF16))
+
+    parts = [mm(wb_ref[...], yn) for yn in yns]
     both = jnp.concatenate(parts, axis=0)
     send_b[...] = jnp.concatenate([both[:, :128], both[:, 128:]], axis=0).astype(BF16)
     chip = q % 8
@@ -240,11 +241,12 @@
 
     keys, queries, values = [], [], []
     for jj in range(2):
-        keys.append(mm(yns[jj], wk).astype(BF16))
-        queries.append(mm(wq_t, yns[jj], TT).astype(BF16))
-        values.append(mm(wv_t, yns[jj], TT).astype(BF16))
-        gate = jax.nn.sigmoid(mm(wgate_t, yns[jj], TT))
+        keys.append(mm(mm(wk_t, yns[jj]).astype(BF16), eye, YN).astype(BF16))
+        queries.append(mm(wq_t, yns[jj]).astype(BF16))
+        values.append(mm(wv_t, yns[jj]).astype(BF16))
+        gate = jax.nn.sigmoid(mm(wgate_t, yns[jj]))
         for half in range(2):
+            pair1[jj, half] = p1s[jj][:, half * 128 : half * 128 + 128].T
             out_gates[jj, half] = gate[:, half * 128 : half * 128 + 128]
 
     head_row = lax.broadcasted_iota(jnp.int32, (128, 256), 0) // 32

time: 42.2 us -> 42.1 us (level)
  no operation moved by 1% of the time
where the time goes in v7:
time: 42.1 us; the launch traced here: 42 us
  Pallas kernels  41.2 us (98%)
  local copies, waits for them, and re-layouts  0.71 us (2%)
    pallas_call x1, Pallas kernels, shards(): pl.pallas_call(kernel, out_shape=jax.ShapeDtypeStruct((512, 128), F32), i...  41.2 us

profile of v7, /device:TPU:1, one launch (start us, length us, event | category | flops | bytes accessed | tf_op | source)
XLA Modules:
  0.0 42.0 jit_solution(10162991048199526774)
XLA Ops:
  0.0 41.2 %shard_map.91 = f32[512,128]{1,0:T(8,128)S(1)} custom-call(bf16[2,2,8,16,128]{4,3,2,1,0:T(8,128)(2,1)} %bitcast.4, s32[2,256]{1,0:T(2,128)} %mask_in.1, bf16[128,256]{1,0:T(8,128)(2,1)} %wl_in.1, bf16[128,256]{1,0:T(8,128)(2,1)} %wr_in.1, bf16[128,128]{1,0:T(8,128)(2,1)} %wg_in.1, bf16[128,128]{1,0:T(8,128)(2,1)} %wo_in.1, bf16[128,512]{1,0:T(8,128)(2,1)} %wa_in.1, ...), custom_call_target="tpu_custom_call" | custom-call | tf_op jit(solution)/shard_map/pallas_call | solution.py:303
  41.3 0.7 %copy.11 = f32[256,2,128]{2,1,0:T(2,128)} copy(f32[256,2,128]{2,1,0:T(2,128)S(1)} %bitcast.3) | data formatting | bytes 524288

commit v8 on v7

--- a/solution.py
+++ b/solution.py
@@ -232,7 +232,7 @@
     both = jnp.concatenate(parts, axis=0)
     send_b[...] = jnp.concatenate([both[:, :128], both[:, 128:]], axis=0).astype(BF16)
     chip = q % 8
-    for step in FAR_ALL:
+    for step in sorted(FAR_ALL, key=lambda v: (-(v[0] + 0.6 * min(v[1], 8 - v[1]) + 1.2 * min(v[2], 4 - v[2])), v)):
         if step[3] == 0:
             send(send_b, have_b.at[core, chip, y], 9 + step[1], at_q[step[0], step[2], 0][1] + y_part[step[1]])
     have_b[core, chip, y] = send_b[...]

time: 42.1 us -> 41.5 us (0.986)
  Pallas kernels: 41.2 us -> 40.7 us
    pallas_call x1, Pallas kernels: 41.2 us -> 40.7 us  [shards(): pl.pallas_call(kernel, out_shape=jax.ShapeDtypeStruct((512, 128), F32), i...]
where the time goes in v8:
time: 41.5 us; the launch traced here: 41.4 us
  Pallas kernels  40.7 us (98%)
  local copies, waits for them, and re-layouts  0.71 us (2%)
    pallas_call x1, Pallas kernels, shards(): pl.pallas_call(kernel, out_shape=jax.ShapeDtypeStruct((512, 128), F32), i...  40.7 us

profile of v8, /device:TPU:1, one launch (start us, length us, event | category | flops | bytes accessed | tf_op | source)
XLA Modules:
  0.0 41.4 jit_solution(1893432296572511570)
XLA Ops:
  0.0 40.7 %shard_map.91 = f32[512,128]{1,0:T(8,128)S(1)} custom-call(bf16[2,2,8,16,128]{4,3,2,1,0:T(8,128)(2,1)} %bitcast.4, s32[2,256]{1,0:T(2,128)} %mask_in.1, bf16[128,256]{1,0:T(8,128)(2,1)} %wl_in.1, bf16[128,256]{1,0:T(8,128)(2,1)} %wr_in.1, bf16[128,128]{1,0:T(8,128)(2,1)} %wg_in.1, bf16[128,128]{1,0:T(8,128)(2,1)} %wo_in.1, bf16[128,512]{1,0:T(8,128)(2,1)} %wa_in.1, ...), custom_call_target="tpu_custom_call" | custom-call | tf_op jit(solution)/shard_map/pallas_call | solution.py:303
  40.7 0.7 %copy.11 = f32[256,2,128]{2,1,0:T(2,128)} copy(f32[256,2,128]{2,1,0:T(2,128)S(1)} %bitcast.3) | data formatting | bytes 524288

commit v9 on v8

--- a/solution.py
+++ b/solution.py
@@ -22,7 +22,7 @@
 FAR_ALL = tuple(
     sorted(
         (s for s in itertools.product(range(2), range(8), range(4), range(2)) if any(s)),
-        key=lambda s: -(s[0] + min(s[1], 8 - s[1]) + min(s[2], 4 - s[2]) + 0.1 * s[3]),
+        key=lambda s: -(s[0] + 0.7 * min(s[1], 8 - s[1]) + min(s[2], 4 - s[2]) + 0.1 * s[3]),
     )
 )
 

time: 41.5 us -> 41.5 us (level)
  no operation moved by 1% of the time
where the time goes in v9:
time: 41.5 us; the launch traced here: 41.3 us
  Pallas kernels  40.6 us (98%)
  local copies, waits for them, and re-layouts  0.71 us (2%)
    pallas_call x1, Pallas kernels, shards(): pl.pallas_call(kernel, out_shape=jax.ShapeDtypeStruct((512, 128), F32), i...  40.6 us

profile of v9, /device:TPU:1, one launch (start us, length us, event | category | flops | bytes accessed | tf_op | source)
XLA Modules:
  0.0 41.3 jit_solution(14700322673403186796)
XLA Ops:
  0.0 40.6 %shard_map.91 = f32[512,128]{1,0:T(8,128)S(1)} custom-call(bf16[2,2,8,16,128]{4,3,2,1,0:T(8,128)(2,1)} %bitcast.4, s32[2,256]{1,0:T(2,128)} %mask_in.1, bf16[128,256]{1,0:T(8,128)(2,1)} %wl_in.1, bf16[128,256]{1,0:T(8,128)(2,1)} %wr_in.1, bf16[128,128]{1,0:T(8,128)(2,1)} %wg_in.1, bf16[128,128]{1,0:T(8,128)(2,1)} %wo_in.1, bf16[128,512]{1,0:T(8,128)(2,1)} %wa_in.1, ...), custom_call_target="tpu_custom_call" | custom-call | tf_op jit(solution)/shard_map/pallas_call | solution.py:303
  40.6 0.7 %copy.11 = f32[256,2,128]{2,1,0:T(2,128)} copy(f32[256,2,128]{2,1,0:T(2,128)S(1)} %bitcast.3) | data formatting | bytes 524288
